TPU v7x, 256 devices: a whole 4x4x8 slice. The times are simulated.
256 devices in a mesh: depth: 32 (over x, y, core), plane: 8 (over z).
Axes of the slice: x: 4, y: 4, z: 8, core: 2. Of those that a mesh axis runs over, the one named last changes fastest.
Arguments:
- spectrum: bfloat16 [2, 1024, 32, 1024], P(None, 'depth', 'plane'), may hold values from -6 to 6
- transfer_coeffs: float32 [8, 4, 4], replicated, may hold values from -3 to 3
- transfer_index: int32 [8], replicated, may hold values from 0 to 7, each once
Outputs:
- scalar_field: float32 [1024, 32, 1024], P('depth', 'plane')
- rendered: float32 [8, 4, 32, 1024], P(None, None, 'plane', 'depth')
Inputs may be any that keep to these rules, and one draw needn't show every extreme that they name: `transfer_index`: each transfer function is used by exactly one image.
All inputs are finite; a program needn't handle non-finite values.
Results may differ from a plain program's by a relative error of at most 0.0003.
Values may be sent and summed in bfloat16 or wider, within the bound.
A program may use at most 64 MiB of HBM per device.

v0:
```python
import functools
import math

import jax
import jax.numpy as jnp
import ml_dtypes
import numpy as np
from jax import lax
from jax.experimental import pallas as pl
from jax.experimental.pallas import tpu as pltpu
from jax.sharding import PartitionSpec as P

NX = 1024
NZ = 1024
density = 2.0
shade_gain = 0.4
tau_scale = density / NZ
f32 = jnp.float32
bf16 = jnp.bfloat16


def split_table(values):
    high = values.astype(ml_dtypes.bfloat16)
    low = (values - high.astype(np.float64)).astype(ml_dtypes.bfloat16)
    return np.stack([high, low])


def x_tables():
    index = np.arange(NX)
    angles = (index[:, None] * index[None, :] % NX) * (2.0 * np.pi / NX)
    return split_table(np.cos(angles) / math.sqrt(NX)), split_table(np.sin(angles) / math.sqrt(NX))


def z_tables():
    q0 = np.arange(256)
    m = np.arange(256)
    tables = []
    for r in range(4):
        angles = (q0[None, :] * (4 * m[:, None] + r) % NZ) * (2.0 * np.pi / NZ)
        tables.append(np.concatenate([np.cos(angles), -np.sin(angles)], axis=1) / math.sqrt(NZ))
    return split_table(np.stack(tables))


def split(value):
    high = lax.reduce_precision(value, 8, 7)
    return high.astype(bf16), (value - high).astype(bf16)


def dot(a, b):
    return jnp.dot(a, b, preferred_element_type=f32)


def residues(re, im):
    a, b = re[0] + re[2], im[0] + im[2]
    c, d = re[0] - re[2], im[0] - im[2]
    e, f = re[1] + re[3], im[1] + im[3]
    g, h = re[1] - re[3], im[1] - im[3]
    return [(a + e, b + f), (c - h, d + g), (a - e, b - f), (c + h, d - g)]


def lighting_kernel_part(field, before, after, r):
    lane = lax.broadcasted_iota(jnp.int32, field.shape, 1)
    up = pltpu.roll(field, 96, 1)
    down = pltpu.roll(field, 32, 1)
    after = pltpu.roll(after, (96 - 32 * r) % 128, 1) if r != 3 else after
    before = pltpu.roll(before, (-32 * r) % 128, 1) if r else before
    up = jnp.where(lane >= 96, after, up)
    down = jnp.where(lane < 32, before, down)
    return 1.0 + shade_gain * jnp.tanh(0.5 * (up - down))


def coefficients(coeff_ref, index_ref):
    row = lax.broadcasted_iota(jnp.int32, (8, 128), 0)
    result = []
    for channel in range(4):
        for n in range(4):
            value = jnp.zeros((8, 128), f32)
            for image in range(8):
                value = jnp.where(row == image, coeff_ref[index_ref[image], channel * 4 + n], value)
            result.append(value)
    return result


def softplus(coeffs, s):
    p = ((coeffs[3] * s + coeffs[2]) * s + coeffs[1]) * s + coeffs[0]
    return jnp.maximum(p, jnp.log(1.0 + jnp.exp(jnp.minimum(p, 80.0))))


def opacity(depth):
    k1, k2, k3 = tau_scale, tau_scale**2 / 2, tau_scale**3 / 6
    small = depth * (k1 - depth * (k2 - depth * k3))
    large = 1.0 - jnp.exp(depth * -tau_scale)
    return jnp.where(depth < 16.0, small, large)


def render_step(coeffs, s, light, state):
    c0, c1, c2, through, depth_sum = state
    depth = softplus(coeffs[12:16], s)
    weight = through * opacity(depth)
    through = through - weight
    weight = weight * light
    c0 = c0 + weight * softplus(coeffs[0:4], s)
    c1 = c1 + weight * softplus(coeffs[4:8], s)
    c2 = c2 + weight * softplus(coeffs[8:12], s)
    return c0, c1, c2, through, depth_sum + depth


def render_kernel(coeff_ref, index_ref, field_ref, before_ref, after_ref, out_ref, light_ref):
    @pl.loop(0, 32)
    def _(step):
        rows = pl.ds(pl.multiple_of(step * 8, 8), 8)
        for r in range(4):
            light_ref[r, rows, :] = lighting_kernel_part(
                field_ref[r, rows, :], before_ref[rows, :], after_ref[rows, :], r
            )

    coeffs = coefficients(coeff_ref, index_ref)

    def body(step, state):
        rows = pl.ds(pl.multiple_of(step * 8, 8), 8)
        for k in range(8):
            for r in range(4):
                s = jnp.broadcast_to(field_ref[r, rows, :][k : k + 1, :], (8, 128))
                light = jnp.broadcast_to(light_ref[r, rows, :][k : k + 1, :], (8, 128))
                state = render_step(coeffs, s, light, state)
        return state

    zero = jnp.zeros((8, 128), f32)
    c0, c1, c2, _, depth_sum = lax.fori_loop(0, 32, body, (zero, zero, zero, zero + 1.0, zero))
    out_ref[0] = c0
    out_ref[1] = c1
    out_ref[2] = c2
    out_ref[3] = jnp.exp(depth_sum * -tau_scale)


def render(coeffs, index, field, before, after):
    smem = pl.BlockSpec(memory_space=pltpu.SMEM)
    vmem = pl.BlockSpec(memory_space=pltpu.VMEM)
    return pl.pallas_call(
        render_kernel,
        out_shape=jax.ShapeDtypeStruct((4, 8, 128), f32),
        in_specs=[smem, smem, vmem, vmem, vmem],
        out_specs=vmem,
        scratch_shapes=[pltpu.VMEM((4, 256, 128), f32)],
    )(coeffs, index, field, before, after)


def body(cos_x, sin_x, table_z, spectrum, transfer_coeffs, transfer_index):
    rows = spectrum.reshape(2, 128, NX)
    cr, ci = rows[0], rows[1]
    h_re = dot(cr, cos_x[0]) + dot(cr, cos_x[1]) - (dot(ci, sin_x[0]) + dot(ci, sin_x[1]))
    h_im = dot(cr, sin_x[0]) + dot(cr, sin_x[1]) + (dot(ci, cos_x[0]) + dot(ci, cos_x[1]))
    h = jnp.stack([h_re, h_im]).reshape(2, 32, 4, NX)
    h = lax.all_to_all(h, "depth", split_axis=3, concat_axis=1, tiled=True)
    h = h.reshape(2, 4, 256, 128)
    field = []
    for r, (re, im) in enumerate(residues(h[0], h[1])):
        high, low = split(jnp.concatenate([re, im]))
        field.append(dot(table_z[0, r], high) + dot(table_z[0, r], low) + dot(table_z[1, r], high))
    field = jnp.stack(field)
    count = lax.axis_size("plane")
    up = [(i, (i + 1) % count) for i in range(count)]
    down = [(j, i) for i, j in up]
    last = jnp.transpose(field[:, :, 96:], (1, 0, 2)).reshape(256, 128)
    first = jnp.transpose(field[:, :, :32], (1, 0, 2)).reshape(256, 128)
    before = lax.ppermute(last, "plane", up)
    after = lax.ppermute(first, "plane", down)
    rendered = render(transfer_coeffs.reshape(8, 16), transfer_index, field, before, after)
    slabs = field.reshape(4, 32, 8, 128)
    slabs = lax.all_to_all(slabs, "depth", split_axis=1, concat_axis=1, tiled=True)
    slabs = slabs.reshape(4, 32, 8, 4, 32)
    scalar_field = jnp.transpose(slabs, (2, 0, 3, 1, 4)).reshape(32, 4, NX)
    rendered = jnp.transpose(rendered.reshape(4, 8, 4, 32), (1, 0, 2, 3))
    return scalar_field, rendered


def solution(mesh):
    cos_x, sin_x = x_tables()
    table_z = z_tables()
    mapped = jax.shard_map(
        body,
        mesh=mesh,
        in_specs=(P(), P(), P(), P(None, "depth", "plane", None), P(), P()),
        out_specs=(P("depth", "plane", None), P(None, None, "plane", "depth")),
        check_vma=False,
    )

    def run(spectrum, transfer_coeffs, transfer_index):
        return mapped(cos_x, sin_x, table_z, spectrum, transfer_coeffs, transfer_index)

    return run
```

profile of v0, /device:TPU:1, one launch (start us, length us, event | category | flops | bytes accessed | tf_op | source)
XLA Modules:
  0.0 124.8 jit_solution(3820813211704837166)
XLA Ops:
  0.6 1.4 %fusion.24 = (bf16[1,32,4,1024]{3,2,1,0:T(4,128)(2,1)S(1)}, bf16[1,32,4,1024]{3,2,1,0:T(4,128)(2,1)S(1)}) fusion(bf16[2,32,4,1024]{3,2,1,0:T(4,128)(2,1)} %param.6), kind=kLoop, calls=%fused_computation.62 | loop fusion | bytes 1048576 | tf_op jit(solution)/shard_map/slice | solution.py:150
  2.8 1.1 copy-done.2
  4.0 1.2 fusion.28
  5.7 1.3 %fusion.29 = f32[1024,128]{0,1:T(8,128)} fusion(bf16[128,1024]{1,0:T(8,128)(2,1)S(1)} %squeeze.31, bf16[1024,1024]{1,0:T(8,128)(2,1)S(1)} %copy-done.1), kind=kOutput, calls=%fused_computation.67 | convolution fusion | flops 268435456 | bytes 2883584 | tf_op jit(solution)/shard_map/dot_general | solution.py:50
  7.9 1.1 copy-done.6
  10.6 2.3 %convolution_add_fusion.1 = f32[1024,128]{0,1:T(8,128)S(1)} fusion(f32[1024,128]{0,1:T(8,128)} %fusion.28, bf16[128,1024]{1,0:T(8,128)(2,1)S(1)} %squeeze.28, bf16[1024,1024]{1,0:T(8,128)(2,1)} %constant.17), kind=kOutput, calls=%fused_computation.4 | convolution fusion | flops 268566528 | bytes 3407872 | tf_op jit(solution)/shard_map/dot_general | solution.py:50
  13.6 1.7 %copy.143 = f32[1,32,4,1024]{1,2,0,3:T(4,128)} copy(f32[1,32,4,1024]{3,2,1,0:T(4,128)S(1)} %stack.35) | data formatting | bytes 1048576 | tf_op jit(solution)/shard_map/stack | solution.py:153
  15.4 4.6 %fusion.25 = f32[1024,2,4,32]{3,2,1,0:T(4,128)} fusion(f32[1,32,4,1024]{1,2,0,3:T(4,128)} %copy.143, f32[1,32,4,1024]{1,2,0,3:T(4,128)S(1)} %copy.142), kind=kLoop, calls=%fused_computation.63 | loop fusion | flops 262144 | bytes 2097152
  20.0 4.4 %reshape.85 = f32[32,1,8192]{2,1,0:T(1,128)S(1)} reshape(f32[1024,2,4,32]{3,2,1,0:T(4,128)} %fusion.25) | data formatting | bytes 2097152
  24.3 25.3 %all_to_all.20 = f32[32,1,8192]{2,1,0:T(1,128)S(1)} all-to-all(f32[32,1,8192]{2,1,0:T(1,128)S(1)} %reshape.85), channel_id=1, replica_groups=mesh['depth'=32,'plane'=8] {'depth'}, dimensions={0} | all-to-all | bytes 2097152 | tf_op jit(solution)/shard_map/all_to_all | solution.py:154
  50.1 3.2 %reduce = f32[32,8192]{1,0:T(8,128)S(1)} reduce(f32[32,1,8192]{2,1,0:T(1,128)S(1)} %all_to_all.20, f32[]{:T(128)} %broadcast), dimensions={1}, to_apply=%all_to_all.14.reduce_sub_computation | reduce | bytes 2097156 | tf_op jit(solution)/shard_map/all_to_all | solution.py:154
  53.4 3.5 %reshape.86 = f32[1024,2,4,32]{3,2,1,0:T(4,128)} reshape(f32[32,8192]{1,0:T(8,128)S(1)} %reduce) | data formatting | bytes 2097152
  56.9 5.6 %copy.188 = f32[2,32,4,32,32]{4,3,1,2,0:T(8,128)} copy(f32[2,32,4,32,32]{1,2,0,4,3:T(4,128)} %bitcast.116) | data formatting | bytes 2097152 | tf_op jit(solution)/shard_map/all_to_all | solution.py:154
  62.5 3.4 %fusion.9 = (f32[1,8,32,4,32]{4,1,2,3,0:T(8,128)S(1)}, f32[1,8,32,4,32]{4,1,2,3,0:T(8,128)S(1)}, f32[1,8,32,4,32]{4,1,2,3,0:T(8,128)}, f32[1,8,32,4,32]{4,1,2,3,0:T(8,128)S(1)}) fusion(f32[2,32,32,4,32]{4,1,2,3,0:T(8,128)} %bitcast.114), kind=kLoop, calls=%fused_computation.42 | loop fusion | flops 327680 | bytes 1572864 | tf_op jit(solution)/shard_map/add | solution.py:58
  66.0 1.1 fusion.15
  68.1 1.2 add.103
  69.3 2.0 %copy.146 = f32[1,8,32,4,32]{2,1,4,3,0:T(8,128)} copy(f32[1,8,32,4,32]{4,1,2,3,0:T(8,128)} %get-tuple-element.2) | data formatting | bytes 262144 | tf_op jit(solution)/shard_map/add | solution.py:58
  71.4 1.2 add.107
  73.1 1.0 copy.150
  74.1 1.2 sub.60
  75.4 2.0 %copy.151 = f32[1,8,32,4,32]{2,1,4,3,0:T(8,128)} copy(f32[1,8,32,4,32]{4,1,2,3,0:T(8,128)} %get-tuple-element.8) | data formatting | bytes 262144 | tf_op jit(solution)/shard_map/add | solution.py:58
  77.4 1.2 add.112
  79.1 1.0 copy.155
  80.2 1.2 sub.65
  83.8 1.2 convolution_add_fusion.10
  86.5 3.9 %all-to-all-start.1 = ((f32[4,32,8,128]{3,2,0,1:T(8,128)}), f32[4,32,8,128]{3,2,0,1:T(8,128)S(1)}, u32[]{:S(2)}, u32[]{:S(2)}) async-start(f32[4,32,8,128]{3,2,0,1:T(8,128)} %pad_maximum_fusion.1), calls=%async_computation.1 | async-start | bytes 1048576 | tf_op jit(solution)/shard_map/all_to_all | solution.py:170
  91.0 1.7 %collective-permute-start = (f32[256,128]{1,0:T(8,128)S(1)}, f32[256,128]{1,0:T(8,128)S(1)}, u32[]{:S(2)}, u32[]{:S(2)}) collective-permute-start(f32[256,128]{1,0:T(8,128)S(1)} %copy.171), channel_id=1, source_target_pairs={{0,1},{1,2},{2,3},{3,4},{4,5},{5,6},{6,7},{7,0},{8,9},{9,10},{10,1... | collective-permute-start | bytes 393224 | tf_op jit(solution)/shard_map/ppermute | solution.py:166
  93.0 4.2 %collective-permute-start.1 = (f32[256,128]{1,0:T(8,128)S(1)}, f32[256,128]{1,0:T(8,128)S(1)}, u32[]{:S(2)}, u32[]{:S(2)}) collective-permute-start(f32[256,128]{1,0:T(8,128)S(1)} %copy.173), channel_id=1, source_target_pairs={{1,0},{2,1},{3,2},{4,3},{5,4},{6,5},{7,6},{0,7},{9,8},{10,9},{11,1... | collective-permute-start | bytes 393224 | tf_op jit(solution)/shard_map/ppermute | solution.py:167
  97.9 2.5 %collective-permute-done.before_ref = f32[256,128]{1,0:T(8,128)S(1)} collective-permute-done((f32[256,128]{1,0:T(8,128)S(1)}, f32[256,128]{1,0:T(8,128)S(1)}, u32[]{:S(2)}, u32[]{:S(2)}) %collective-permute-start) | collective-permute-done | bytes 131104 | tf_op jit(solution)/shard_map/ppermute | solution.py:166
  101.7 15.0 %shard_map.77 = f32[4,8,128]{2,1,0:T(8,128)} custom-call(f32[8,16]{1,0:T(8,128)} %copy.174.coeff_ref, s32[8]{0:T(128)} %index_ref.1, f32[4,256,128]{2,1,0:T(8,128)} %copy-done.3, f32[256,128]{1,0:T(8,128)} %copy-done.15, f32[256,128]{1,0:T(8,128)} %copy-done.16), custom_call_target="tpu_custom_call" | custom-call | tf_op jit(solution)/shard_map/pallas_call | solution.py:139
  119.1 2.5 %copy.169 = f32[8,4,4,32,32]{4,3,2,1,0:T(8,128)} copy(f32[8,4,4,32,32]{4,2,0,1,3:T(4,128)S(1)} %bitcast.117) | data formatting | bytes 1048576 | tf_op jit(solution)/shard_map/transpose | solution.py:172
  121.6 3.1 %reshape.80 = f32[32,4,1024]{2,1,0:T(4,128)} reshape(f32[8,4,4,32,32]{4,3,2,1,0:T(8,128)} %copy.169) | data formatting | bytes 1048576 | tf_op jit(solution)/shard_map/reshape | solution.py:172
  (84 shorter events, 16.0 us)
Async XLA Ops:
  0.6 1.8 %copy-start.1 = (bf16[1024,1024]{1,0:T(8,128)(2,1)S(1)}, bf16[1024,1024]{1,0:T(8,128)(2,1)}, u32[]{:S(2)}) copy-start(bf16[1024,1024]{1,0:T(8,128)(2,1)} %constant.11) | copy-start | bytes 6291460
  2.4 1.6 %copy-start.2 = (bf16[1024,1024]{1,0:T(8,128)(2,1)S(1)}, bf16[1024,1024]{1,0:T(8,128)(2,1)}, u32[]{:S(2)}) copy-start(bf16[1024,1024]{1,0:T(8,128)(2,1)} %constant.15) | copy-start | bytes 6291460
  5.7 1.8 %copy-start.4 = (bf16[1024,1024]{1,0:T(8,128)(2,1)S(1)}, bf16[1024,1024]{1,0:T(8,128)(2,1)}, u32[]{:S(2)}) copy-start(bf16[1024,1024]{1,0:T(8,128)(2,1)} %constant.13) | copy-start | bytes 6291460
  7.4 1.6 %copy-start.6 = (bf16[1024,1024]{1,0:T(8,128)(2,1)S(1)}, bf16[1024,1024]{1,0:T(8,128)(2,1)}, u32[]{:S(2)}) copy-start(bf16[1024,1024]{1,0:T(8,128)(2,1)} %constant.17) | copy-start | bytes 6291460
  10.5 2.4 %copy-start.5 = (bf16[1024,1024]{1,0:T(8,128)(2,1)S(1)}, bf16[1024,1024]{1,0:T(8,128)(2,1)}, u32[]{:S(2)}) copy-start(bf16[1024,1024]{1,0:T(8,128)(2,1)} %constant.13) | copy-start | bytes 6291460
  10.5 2.5 %copy-start.7 = (f32[1024,128]{0,1:T(8,128)S(1)}, f32[1024,128]{0,1:T(8,128)}, u32[]{:S(2)}) copy-start(f32[1024,128]{0,1:T(8,128)} %fusion.29) | copy-start | bytes 1572868
  62.5 3.5 %copy-start = (f32[2,32,4,32,32]{4,3,1,2,0:T(8,128)S(1)}, f32[2,32,4,32,32]{4,3,1,2,0:T(8,128)}, u32[]{:S(2)}) copy-start(f32[2,32,4,32,32]{4,3,1,2,0:T(8,128)} %copy.188) | copy-start | bytes 3145732
  67.1 5.5 %copy-start.11 = (bf16[256,512]{1,0:T(8,128)(2,1)S(1)}, bf16[256,512]{1,0:T(8,128)(2,1)}, u32[]{:S(2)}) copy-start(bf16[256,512]{1,0:T(8,128)(2,1)} %constant.19) | copy-start | bytes 786436
  73.1 5.6 %copy-start.10 = (bf16[256,512]{1,0:T(8,128)(2,1)S(1)}, bf16[256,512]{1,0:T(8,128)(2,1)}, u32[]{:S(2)}) copy-start(bf16[256,512]{1,0:T(8,128)(2,1)} %constant.23) | copy-start | bytes 786436
  79.1 2.7 %copy-start.9 = (bf16[256,512]{1,0:T(8,128)(2,1)S(1)}, bf16[256,512]{1,0:T(8,128)(2,1)}, u32[]{:S(2)}) copy-start(bf16[256,512]{1,0:T(8,128)(2,1)} %constant.27) | copy-start | bytes 786436
  82.3 1.0 copy-start.8
  82.8 2.2 %copy-start.14 = (bf16[256,512]{1,0:T(8,128)(2,1)S(1)}, bf16[256,512]{1,0:T(8,128)(2,1)}, u32[]{:S(2)}) copy-start(bf16[256,512]{1,0:T(8,128)(2,1)} %constant.25) | copy-start | bytes 786436
  83.1 2.1 %copy-start.13 = (bf16[256,512]{1,0:T(8,128)(2,1)S(1)}, bf16[256,512]{1,0:T(8,128)(2,1)}, u32[]{:S(2)}) copy-start(bf16[256,512]{1,0:T(8,128)(2,1)} %constant.29) | copy-start | bytes 786436
  83.2 2.2 %copy-start.12 = (bf16[256,512]{1,0:T(8,128)(2,1)S(1)}, bf16[256,512]{1,0:T(8,128)(2,1)}, u32[]{:S(2)}) copy-start(bf16[256,512]{1,0:T(8,128)(2,1)} %constant.33) | copy-start | bytes 786436
  86.5 31.6 %all-to-all-start.1 = ((f32[4,32,8,128]{3,2,0,1:T(8,128)}), f32[4,32,8,128]{3,2,0,1:T(8,128)S(1)}, u32[]{:S(2)}, u32[]{:S(2)}) async-start(f32[4,32,8,128]{3,2,0,1:T(8,128)} %pad_maximum_fusion.1), calls=%async_computation.1 | async-start | bytes 1048576 | tf_op jit(solution)/shard_map/all_to_all | solution.py:170
  90.5 9.9 %copy-start.3 = (f32[4,256,128]{2,1,0:T(8,128)}, f32[4,256,128]{2,1,0:T(8,128)S(1)}, u32[]{:S(2)}) copy-start(f32[4,256,128]{2,1,0:T(8,128)S(1)} %pad_maximum_fusion.2.field_ref) | copy-start | bytes 1572868
  90.5 6.7 %copy-start.17 = (f32[8,4,4]{0,2,1:T(4,128)S(1)}, f32[8,4,4]{0,2,1:T(4,128)}, u32[]{:S(2)}) copy-start(f32[8,4,4]{0,2,1:T(4,128)} %param.7) | copy-start | bytes 1540
  91.0 9.4 %collective-permute-start = (f32[256,128]{1,0:T(8,128)S(1)}, f32[256,128]{1,0:T(8,128)S(1)}, u32[]{:S(2)}, u32[]{:S(2)}) collective-permute-start(f32[256,128]{1,0:T(8,128)S(1)} %copy.171), channel_id=1, source_target_pairs={{0,1},{1,2},{2,3},{3,4},{4,5},{5,6},{6,7},{7,0},{8,9},{9,10},{10,1... | collective-permute-start | bytes 393224 | tf_op jit(solution)/shard_map/ppermute | solution.py:166
  93.0 7.4 %collective-permute-start.1 = (f32[256,128]{1,0:T(8,128)S(1)}, f32[256,128]{1,0:T(8,128)S(1)}, u32[]{:S(2)}, u32[]{:S(2)}) collective-permute-start(f32[256,128]{1,0:T(8,128)S(1)} %copy.173), channel_id=1, source_target_pairs={{1,0},{2,1},{3,2},{4,3},{5,4},{6,5},{7,6},{0,7},{9,8},{10,9},{11,1... | collective-permute-start | bytes 393224 | tf_op jit(solution)/shard_map/ppermute | solution.py:167
  100.4 0.7 copy-start.15
  101.1 0.6 copy-start.16
where the time goes:
time: 126 us; the launch traced here: 125 us
  local copies, waits for them, and re-layouts  47.1 us (37%)
  blocking collectives  25.3 us (20%)
  Pallas kernels  15 us (12%)
  other arithmetic  13.2 us (10%)
  matrix products  10.7 us (8%)
  starting transfers between devices  9.91 us (8%)
  waiting for transfers between devices  2.48 us (2%)
    all_to_all x1, blocking collectives, body(): h = lax.all_to_all(h, 'depth', split_axis=3, concat_axis=1, tiled=True)  25.3 us
    pallas_call x1, Pallas kernels, render(): pl.pallas_call(render_kernel, out_shape=jax.ShapeDtypeStruct((4, 8, 128),...  15 us
    unnamed x42, local copies, waits for them, and re-layouts  12.6 us
    dot_general x20, matrix products, dot(): return jnp.dot(a, b, preferred_element_type=f32)  10.7 us
    add x8, local copies, waits for them, and re-layouts, residues(): return [(a + e, b + f), (c - h, d + g), (a - e, b - f), (c + h, d - g)]  9.19 us
    all_to_all x2, local copies, waits for them, and re-layouts, body(): h = lax.all_to_all(h, 'depth', split_axis=3, concat_axis=1, tiled=True)  6.1 us
    sub x8, local copies, waits for them, and re-layouts, residues(): return [(a + e, b + f), (c - h, d + g), (a - e, b - f), (c + h, d - g)]  5.33 us
    unnamed x1, other arithmetic  4.6 us
  transfers between devices with their start and end apart: 3, of which 1 were waited for; matrix products, arithmetic and copies ran while one was open for 2% of the time, Pallas kernels for 12%

commit v1 on v0

v1 whole, which is shorter than its diff:
```python
import math

import jax
import jax.numpy as jnp
import ml_dtypes
import numpy as np
from jax import lax
from jax.experimental import pallas as pl
from jax.experimental.pallas import tpu as pltpu
from jax.sharding import PartitionSpec as P

NX = 1024
NZ = 1024
density = 2.0
shade_gain = 0.4
tau_scale = density / NZ
f32 = jnp.float32
bf16 = jnp.bfloat16
MESH = pl.DeviceIdType.MESH


def split_table(values):
    high = values.astype(ml_dtypes.bfloat16)
    low = (values - high.astype(np.float64)).astype(ml_dtypes.bfloat16)
    return np.stack([high, low])


def x_table():
    index = np.arange(NX)
    angles = (index[:, None] * index[None, :] % NX) * (2.0 * np.pi / NX)
    tables = [split_table(t / math.sqrt(NX)).reshape(2, NX, 8, 128) for t in (np.cos(angles), np.sin(angles))]
    return np.ascontiguousarray(np.concatenate(tables, axis=3).transpose(2, 0, 1, 3))


def z_table():
    q0 = np.arange(256)
    m = np.arange(256)
    tables = []
    for r in range(4):
        angles = (q0[None, :] * (4 * m[:, None] + r) % NZ) * (2.0 * np.pi / NZ)
        table = np.concatenate([np.cos(angles), -np.sin(angles)], axis=1) / math.sqrt(NZ)
        tables.append(split_table(table).reshape(512, 512))
    return np.stack(tables)


def split(value):
    high = value.astype(bf16)
    return high, (value - high.astype(f32)).astype(bf16)


def dot(a, b):
    return jnp.dot(a, b, preferred_element_type=f32)


def residues(re, im):
    a, b = re[0] + re[2], im[0] + im[2]
    c, d = re[0] - re[2], im[0] - im[2]
    e, f = re[1] + re[3], im[1] + im[3]
    g, h = re[1] - re[3], im[1] - im[3]
    return [(a + e, b + f), (c - h, d + g), (a - e, b - f), (c + h, d - g)]


def lighting(field, before, after, r):
    lane = lax.broadcasted_iota(jnp.int32, field.shape, 1)
    up = pltpu.roll(field, 96, 1)
    down = pltpu.roll(field, 32, 1)
    after = pltpu.roll(after, (96 - 32 * r) % 128, 1) if r != 3 else after
    before = pltpu.roll(before, (-32 * r) % 128, 1) if r else before
    up = jnp.where(lane >= 96, after, up)
    down = jnp.where(lane < 32, before, down)
    return 1.0 + shade_gain * jnp.tanh(0.5 * (up - down))


def coefficients(coeff_ref, index_ref):
    row = lax.broadcasted_iota(jnp.int32, (8, 128), 0)
    result = []
    for channel in range(4):
        for n in range(4):
            value = jnp.zeros((8, 128), f32)
            for image in range(8):
                value = jnp.where(row == image, coeff_ref[index_ref[image], channel * 4 + n], value)
            result.append(value)
    return result


def softplus(coeffs, s):
    p = ((coeffs[3] * s + coeffs[2]) * s + coeffs[1]) * s + coeffs[0]
    return jnp.maximum(p, jnp.log(1.0 + jnp.exp(jnp.minimum(p, 80.0))))


def opacity(depth):
    k1, k2, k3 = tau_scale, tau_scale**2 / 2, tau_scale**3 / 6
    small = depth * (k1 - depth * (k2 - depth * k3))
    large = 1.0 - jnp.exp(depth * -tau_scale)
    return jnp.where(depth < 16.0, small, large)


def render_step(coeffs, s, light, state):
    c0, c1, c2, through, depth_sum = state
    depth = softplus(coeffs[12:16], s)
    weight = through * opacity(depth)
    through = through - weight
    weight = weight * light
    c0 = c0 + weight * softplus(coeffs[0:4], s)
    c1 = c1 + weight * softplus(coeffs[4:8], s)
    c2 = c2 + weight * softplus(coeffs[8:12], s)
    return c0, c1, c2, through, depth_sum + depth


def shuffle(parts, place):
    group = lax.broadcasted_iota(jnp.int32, parts[0].shape, 1) // 32
    result = None
    for g in range(4):
        shift = (32 * (g - place)) % 128
        moved = pltpu.roll(parts[g], shift, 1) if shift else parts[g]
        result = moved if result is None else jnp.where(group == g, moved, result)
    return result


def kernel(
    coeff_ref, index_ref, spectrum_ref, x_hbm, z_hbm,
    field_out, image_out,
    x_ref, z_ref, mode_ref, send_ref, recv_ref, pair_ref, field_ref, light_ref, pack_ref, halo_ref, slab_ref,
    x_sem, z_sem, send_sem, recv_sem, halo_send, halo_recv, slab_send, slab_recv,
):
    me = lax.axis_index("depth")
    plane = lax.axis_index("plane")
    planes = lax.axis_size("plane")
    next_plane = lax.rem(plane + 1, planes)
    last_plane = lax.rem(plane + planes - 1, planes)

    def chunk_of(step):
        return lax.rem(me // 4 + step, 8)

    def x_copy(step):
        chunk = chunk_of(step)
        return pltpu.make_async_copy(x_hbm.at[chunk], x_ref.at[chunk], x_sem.at[step])

    z_copy = pltpu.make_async_copy(z_hbm, z_ref, z_sem)

    @pl.loop(0, 8)
    def _(step):
        x_copy(step).start()

    z_copy.start()

    barrier = pltpu.get_barrier_semaphore()

    @pl.loop(1, 32)
    def _(step):
        pl.semaphore_signal(barrier, inc=1, device_id={"depth": lax.rem(me + step, 32)}, device_id_type=MESH)

    pl.semaphore_signal(barrier, inc=1, device_id={"plane": next_plane}, device_id_type=MESH)
    pl.semaphore_signal(barrier, inc=1, device_id={"plane": last_plane}, device_id_type=MESH)

    def mode_send(to):
        return pltpu.make_async_remote_copy(
            src_ref=send_ref.at[to], dst_ref=recv_ref.at[me], send_sem=send_sem.at[to], recv_sem=recv_sem.at[me],
            device_id={"depth": to}, device_id_type=MESH,
        )

    def mode_recv(source):
        return pltpu.make_async_remote_copy(
            src_ref=send_ref.at[source], dst_ref=recv_ref.at[source], send_sem=send_sem.at[source],
            recv_sem=recv_sem.at[source], device_id={"depth": source}, device_id_type=MESH,
        )

    def mode_keep():
        return pltpu.make_async_copy(send_ref.at[me], recv_ref.at[me], recv_sem.at[me])

    @pl.loop(0, 8)
    def _(step):
        chunk = chunk_of(step)
        x_copy(step).wait()
        modes = spectrum_ref[...]
        waves = dot(modes, x_ref[chunk, 0]) + dot(modes, x_ref[chunk, 1])
        mode_ref[0] = waves[:128, :128] - waves[128:, 128:]
        mode_ref[1] = waves[:128, 128:] + waves[128:, :128]
        for part in range(2):
            rows = [mode_ref[part, pl.ds(y, 32, stride=4), :] for y in range(4)]
            for d in range(4):
                send_ref[chunk * 4 + d, part] = shuffle(rows, d)

        @pl.when(step == 0)
        def _():
            pl.semaphore_wait(barrier, 33)

        @pl.loop(0, 4)
        def _(d):
            to = chunk * 4 + d

            @pl.when(to != me)
            def _():
                mode_send(to).start()

            @pl.when(to == me)
            def _():
                mode_keep().start()

    @pl.loop(0, 8)
    def _(s):
        @pl.loop(0, 4)
        def _(j):
            source = s + 8 * j

            @pl.when(source != me)
            def _():
                mode_recv(source).wait_recv()

            @pl.when(source == me)
            def _():
                mode_keep().wait()

        re = [recv_ref[s + 8 * j, 0] for j in range(4)]
        im = [recv_ref[s + 8 * j, 1] for j in range(4)]
        for r, pair in enumerate(residues(re, im)):
            for part in range(2):
                high, low = split(pair[part])
                rows = pl.ds(pl.multiple_of(part * 256 + s * 32, 32), 32)
                pair_ref[r, rows, 0:128] = high
                pair_ref[r, rows, 128:256] = low

    z_copy.wait()

    @pl.loop(0, 4)
    def _(r):
        p = dot(z_ref[r], pair_ref[r])
        field_ref[r] = (p[:256, :128] + p[:256, 128:]) + (p[256:, :128] + p[256:, 128:])

    @pl.loop(0, 32)
    def _(step):
        rows = pl.ds(pl.multiple_of(step * 8, 8), 8)
        parts = [field_ref[r, rows, :] for r in range(4)]
        pack_ref[0, rows, :] = shuffle(parts, 3)
        pack_ref[1, rows, :] = shuffle(parts, 0)

    halos = [
        pltpu.make_async_remote_copy(
            src_ref=pack_ref.at[side], dst_ref=halo_ref.at[side], send_sem=halo_send.at[side],
            recv_sem=halo_recv.at[side], device_id={"plane": to}, device_id_type=MESH,
        )
        for side, to in ((0, next_plane), (1, last_plane))
    ]
    for halo in halos:
        halo.start()

    def own_rows(slab):
        return field_ref.at[:, pl.ds(pl.multiple_of(slab * 8, 8), 8), :]

    def slab_send_copy(to):
        return pltpu.make_async_remote_copy(
            src_ref=own_rows(to), dst_ref=slab_ref.at[me], send_sem=slab_send.at[to], recv_sem=slab_recv.at[me],
            device_id={"depth": to}, device_id_type=MESH,
        )

    def slab_recv_copy(source):
        return pltpu.make_async_remote_copy(
            src_ref=own_rows(source), dst_ref=slab_ref.at[source], send_sem=slab_send.at[source],
            recv_sem=slab_recv.at[source], device_id={"depth": source}, device_id_type=MESH,
        )

    slab_keep = pltpu.make_async_copy(own_rows(me), slab_ref.at[me], slab_recv.at[me])
    slab_keep.start()

    @pl.loop(1, 32)
    def _(step):
        slab_send_copy(lax.rem(me + step, 32)).start()

    coeffs = coefficients(coeff_ref, index_ref)
    for halo in halos:
        halo.wait_recv()

    @pl.loop(0, 32)
    def _(step):
        rows = pl.ds(pl.multiple_of(step * 8, 8), 8)
        for r in range(4):
            light_ref[r, rows, :] = lighting(field_ref[r, rows, :], halo_ref[0, rows, :], halo_ref[1, rows, :], r)

    def body(step, state):
        rows = pl.ds(pl.multiple_of(step * 8, 8), 8)
        for k in range(8):
            for r in range(4):
                s = jnp.broadcast_to(field_ref[r, rows, :][k : k + 1, :], (8, 128))
                light = jnp.broadcast_to(light_ref[r, rows, :][k : k + 1, :], (8, 128))
                state = render_step(coeffs, s, light, state)
        return state

    zero = jnp.zeros((8, 128), f32)
    c0, c1, c2, _, depth_sum = lax.fori_loop(0, 32, body, (zero, zero, zero, zero + 1.0, zero))
    image_out[0] = c0
    image_out[1] = c1
    image_out[2] = c2
    image_out[3] = jnp.exp(depth_sum * -tau_scale)

    slab_keep.wait()

    @pl.loop(1, 32)
    def _(step):
        slab_recv_copy(lax.rem(me + step, 32)).wait_recv()

    @pl.loop(0, 8)
    def _(g):
        for r in range(4):
            parts = [slab_ref[g * 4 + d, r] for d in range(4)]
            for y in range(4):
                field_out[pl.ds(r * 32 + g * 4 + y, 8, stride=128), :] = shuffle(parts, y)

    @pl.loop(1, 32)
    def _(step):
        to = lax.rem(me + step, 32)
        mode_send(to).wait_send()
        slab_send_copy(to).wait_send()

    for halo in halos:
        halo.wait_send()


def body(x_tab, z_tab, spectrum, transfer_coeffs, transfer_index):
    smem = pl.BlockSpec(memory_space=pltpu.SMEM)
    vmem = pl.BlockSpec(memory_space=pltpu.VMEM)
    hbm = pl.BlockSpec(memory_space=pl.ANY)
    sem = pltpu.SemaphoreType.DMA
    field, image = pl.pallas_call(
        kernel,
        out_shape=[jax.ShapeDtypeStruct((1024, 128), f32), jax.ShapeDtypeStruct((4, 8, 128), f32)],
        in_specs=[smem, smem, vmem, hbm, hbm],
        out_specs=[vmem, vmem],
        scratch_shapes=[
            pltpu.VMEM((8, 2, NX, 256), bf16),
            pltpu.VMEM((4, 512, 512), bf16),
            pltpu.VMEM((2, 128, 128), f32),
            pltpu.VMEM((32, 2, 32, 128), f32),
            pltpu.VMEM((32, 2, 32, 128), f32),
            pltpu.VMEM((4, 512, 256), bf16),
            pltpu.VMEM((4, 256, 128), f32),
            pltpu.VMEM((4, 256, 128), f32),
            pltpu.VMEM((2, 256, 128), f32),
            pltpu.VMEM((2, 256, 128), f32),
            pltpu.VMEM((32, 4, 8, 128), f32),
            sem((8,)), sem, sem((32,)), sem((32,)), sem((2,)), sem((2,)), sem((32,)), sem((32,)),
        ],
        compiler_params=pltpu.CompilerParams(
            collective_id=0, has_side_effects=True, vmem_limit_bytes=40 * 2**20
        ),
    )(transfer_coeffs.reshape(8, 16), transfer_index, spectrum.reshape(256, NX), x_tab, z_tab)
    scalar_field = field.reshape(32, 8, 4, 128).transpose(0, 2, 1, 3).reshape(32, 4, NX)
    rendered = jnp.transpose(image.reshape(4, 8, 4, 32), (1, 0, 2, 3))
    return scalar_field, rendered


def solution(mesh):
    x_tab, z_tab = x_table(), z_table()
    mapped = jax.shard_map(
        body,
        mesh=mesh,
        in_specs=(P(), P(), P(None, "depth", "plane", None), P(), P()),
        out_specs=(P("depth", "plane", None), P(None, None, "plane", "depth")),
        check_vma=False,
    )

    def run(spectrum, transfer_coeffs, transfer_index):
        return mapped(x_tab, z_tab, spectrum, transfer_coeffs, transfer_index)

    return run
```

time: 126 us -> 65.2 us (0.52)
  Pallas kernels: 15 us -> 54.4 us
  local copies, waits for them, and re-layouts: 47.1 us -> 9.08 us
  blocking collectives: 25.3 us -> 0 us
  other arithmetic: 13.2 us -> 0 us
  matrix products: 10.7 us -> 0 us
  starting transfers between devices: 9.91 us -> 0 us
  waiting for transfers between devices: 2.48 us -> 0 us
    pallas_call x1, Pallas kernels: 15 us -> 54.4 us  [body(): pl.pallas_call(kernel, out_shape=[jax.ShapeDtypeStruct((1024, 128), f32),...]
    all_to_all x1 -> x0, blocking collectives: 25.3 us -> none  [body(): h = lax.all_to_all(h, 'depth', split_axis=3, concat_axis=1, tiled=True)]
    dot_general x20 -> x0, matrix products: 10.7 us -> none  [dot(): return jnp.dot(a, b, preferred_element_type=f32)]
    add x8 -> x0, local copies, waits for them, and re-layouts: 9.19 us -> none  [residues(): return [(a + e, b + f), (c - h, d + g), (a - e, b - f), (c + h, d - g)]]
    unnamed x42 -> x7, local copies, waits for them, and re-layouts: 12.6 us -> 6.42 us
    all_to_all x2 -> x0, local copies, waits for them, and re-layouts: 6.1 us -> none  [body(): h = lax.all_to_all(h, 'depth', split_axis=3, concat_axis=1, tiled=True)]
    ppermute x2 -> x0, starting transfers between devices: 5.96 us -> none  [the longest x1 4.24 us: body(): after = lax.ppermute(first, 'plane', down)]
    sub x8 -> x0, local copies, waits for them, and re-layouts: 5.33 us -> none  [residues(): return [(a + e, b + f), (c - h, d + g), (a - e, b - f), (c + h, d - g)]]
  transfers between devices with their start and end apart: 3 -> 0, of which waited for: 1 -> 0; matrix products, arithmetic and copies ran while one was open for 2% -> 0% of each run, Pallas kernels for 12% -> 0%
where the time goes in v1:
time: 65.2 us; the launch traced here: 64.2 us
  Pallas kernels  54.4 us (83%)
  local copies, waits for them, and re-layouts  9.08 us (14%)
  between operations  0.66 us (1%)
    pallas_call x1, Pallas kernels, body(): pl.pallas_call(kernel, out_shape=[jax.ShapeDtypeStruct((1024, 128), f32),...  54.4 us
    unnamed x7, local copies, waits for them, and re-layouts  6.42 us

profile of v1, /device:TPU:1, one launch (start us, length us, event | category | flops | bytes accessed | tf_op | source)
XLA Modules:
  0.0 64.2 jit_solution(17860258129256687073)
XLA Ops:
  0.6 0.8 %copy.7.coeff_ref = f32[8,16]{1,0:T(8,128)S(1)} copy(f32[8,16]{0,1:T(8,128)} %bitcast.11) | data formatting | bytes 1024 | tf_op jit(solution)/shard_map/reshape | solution.py:345
  1.4 1.2 %reshape.20.spectrum_ref = bf16[256,1024]{1,0:T(8,128)(2,1)S(1)} reshape(bf16[2,32,4,1024]{3,2,1,0:T(4,128)(2,1)} %param.5) | data formatting | bytes 1048576 | tf_op jit(solution)/shard_map/reshape | solution.py:345
  2.6 0.0 copy-start
  2.6 3.4 %copy-done = bf16[8,2,1024,256]{3,2,1,0:T(8,128)(2,1)S(1)} copy-done((bf16[8,2,1024,256]{3,2,1,0:T(8,128)(2,1)S(1)}, bf16[8,2,1024,256]{3,2,1,0:T(8,128)(2,1)}, u32[]{:S(2)}) %copy-start) | copy-done | bytes 8388632
  6.0 0.0 copy-start.1
  6.0 1.6 %copy-done.1 = bf16[4,512,512]{2,1,0:T(8,128)(2,1)S(1)} copy-done((bf16[4,512,512]{2,1,0:T(8,128)(2,1)S(1)}, bf16[4,512,512]{2,1,0:T(8,128)(2,1)}, u32[]{:S(2)}) %copy-start.1) | copy-done | bytes 2097176
  7.5 0.0 copy-start.2
  7.5 0.7 %copy-done.2 = s32[8]{0:T(128)S(1)} copy-done((s32[8]{0:T(128)S(1)}, s32[8]{0:T(128)}, u32[]{:S(2)}) %copy-start.2) | copy-done | bytes 56
  8.2 54.4 %shard_map.68 = (f32[1024,128]{1,0:T(8,128)S(1)}, f32[4,8,128]{2,1,0:T(8,128)S(1)}) custom-call(f32[8,16]{1,0:T(8,128)S(1)} %copy.7.coeff_ref, s32[8]{0:T(128)S(1)} %copy-done.2, bf16[256,1024]{1,0:T(8,128)(2,1)S(1)} %reshape.20.spectrum_ref, bf16[8,2,1024,256]{3,2,1,0:T(8,128)(2,1)S(1)} %copy-done, bf16[4,512,512]{2,1,0:T(8,128)(2,1)S(1)} %copy-done.1), custom_call_target="tpu_custom_call" | custom-call | tf_op jit(solution)/shard_map/pallas_call | solution.py:323
  62.7 0.1 reshape.23
  62.8 0.6 %copy.11 = f32[4,8,4,32]{3,2,0,1:T(4,128)} copy(f32[4,8,4,32]{3,2,1,0:T(4,128)S(1)} %reshape.23) | data formatting | bytes 32768 | tf_op jit(solution)/shard_map/reshape | solution.py:347
  63.4 0.8 %copy.13 = f32[32,4,1024]{2,1,0:T(4,128)} copy(f32[32,4,1024]{2,1,0:T(4,128)S(1)} %bitcast.9) | data formatting | bytes 1048576
Async XLA Ops:
  2.6 3.4 %copy-start = (bf16[8,2,1024,256]{3,2,1,0:T(8,128)(2,1)S(1)}, bf16[8,2,1024,256]{3,2,1,0:T(8,128)(2,1)}, u32[]{:S(2)}) copy-start(bf16[8,2,1024,256]{3,2,1,0:T(8,128)(2,1)} %constant.4.clone.x_hbm) | copy-start | bytes 25165828
  6.0 1.6 %copy-start.1 = (bf16[4,512,512]{2,1,0:T(8,128)(2,1)S(1)}, bf16[4,512,512]{2,1,0:T(8,128)(2,1)}, u32[]{:S(2)}) copy-start(bf16[4,512,512]{2,1,0:T(8,128)(2,1)} %constant.5.clone.z_hbm) | copy-start | bytes 6291460
  7.5 0.7 %copy-start.2 = (s32[8]{0:T(128)S(1)}, s32[8]{0:T(128)}, u32[]{:S(2)}) copy-start(s32[8]{0:T(128)} %index_ref.1) | copy-start | bytes 100

commit v2 on v1

--- a/solution.py
+++ b/solution.py
@@ -14,6 +14,7 @@
 density = 2.0
 shade_gain = 0.4
 tau_scale = density / NZ
+LN2 = math.log(2.0)
 f32 = jnp.float32
 bf16 = jnp.bfloat16
 MESH = pl.DeviceIdType.MESH
@@ -78,9 +79,26 @@
         for n in range(4):
             value = jnp.zeros((8, 128), f32)
             for image in range(8):
-                value = jnp.where(row == image, coeff_ref[index_ref[image], channel * 4 + n], value)
+                value = jnp.where(row == image, coeff_ref[channel, n, index_ref[image]], value)
             result.append(value)
     return result
+
+
+def encode(parts):
+    peak = jnp.maximum(jnp.abs(parts[0]), jnp.abs(parts[1]))
+    peak = jnp.maximum(jnp.max(peak, axis=0, keepdims=True), 1e-30)
+    level = jnp.floor(jnp.log(peak) * (256.0 / LN2)) + 2.0
+    level = jnp.broadcast_to(level, (16, 128))
+    scale = jnp.exp2(level[:8] * (-1.0 / 256.0)) * 32766.0
+    scale = jnp.concatenate([scale] * 4)
+    codes = [jnp.round(part * scale).astype(jnp.int32).astype(jnp.int16) for part in parts]
+    return codes, level.astype(jnp.int32).astype(jnp.int16)
+
+
+def decode(codes, level):
+    step = jnp.exp2(level.astype(jnp.int32).astype(f32)[:8] * (1.0 / 256.0)) * (1.0 / 32766.0)
+    step = jnp.concatenate([step] * 4)
+    return [code.astype(jnp.int32).astype(f32) * step for code in codes]
 
 
 def softplus(coeffs, s):
@@ -120,7 +138,7 @@
 def kernel(
     coeff_ref, index_ref, spectrum_ref, x_hbm, z_hbm,
     field_out, image_out,
-    x_ref, z_ref, mode_ref, send_ref, recv_ref, pair_ref, field_ref, light_ref, pack_ref, halo_ref, slab_ref,
+    row_ref, x_ref, z_ref, mode_ref, send_ref, recv_ref, pair_ref, field_ref, light_ref, pack_ref, halo_ref, slab_ref,
     x_sem, z_sem, send_sem, recv_sem, halo_send, halo_recv, slab_send, slab_recv,
 ):
     me = lax.axis_index("depth")
@@ -168,18 +186,26 @@
     def mode_keep():
         return pltpu.make_async_copy(send_ref.at[me], recv_ref.at[me], recv_sem.at[me])
 
+    row_ref[...] = spectrum_ref[...].reshape(256, NX)
+
     @pl.loop(0, 8)
     def _(step):
         chunk = chunk_of(step)
         x_copy(step).wait()
-        modes = spectrum_ref[...]
+        modes = row_ref[...]
         waves = dot(modes, x_ref[chunk, 0]) + dot(modes, x_ref[chunk, 1])
         mode_ref[0] = waves[:128, :128] - waves[128:, 128:]
         mode_ref[1] = waves[:128, 128:] + waves[128:, :128]
+        parts = [[] for _ in range(4)]
         for part in range(2):
             rows = [mode_ref[part, pl.ds(y, 32, stride=4), :] for y in range(4)]
             for d in range(4):
-                send_ref[chunk * 4 + d, part] = shuffle(rows, d)
+                parts[d].append(shuffle(rows, d))
+        for d in range(4):
+            codes, level = encode(parts[d])
+            send_ref[chunk * 4 + d, 0:32] = codes[0]
+            send_ref[chunk * 4 + d, 32:64] = codes[1]
+            send_ref[chunk * 4 + d, 64:80] = level
 
         @pl.when(step == 0)
         def _():
@@ -211,8 +237,12 @@
             def _():
                 mode_keep().wait()
 
-        re = [recv_ref[s + 8 * j, 0] for j in range(4)]
-        im = [recv_ref[s + 8 * j, 1] for j in range(4)]
+        re, im = [], []
+        for j in range(4):
+            got = recv_ref.at[s + 8 * j]
+            real, imag = decode([got[0:32], got[32:64]], got[64:80])
+            re.append(real)
+            im.append(imag)
         for r, pair in enumerate(residues(re, im)):
             for part in range(2):
                 high, low = split(pair[part])
@@ -260,18 +290,19 @@
         )
 
     slab_keep = pltpu.make_async_copy(own_rows(me), slab_ref.at[me], slab_recv.at[me])
-    slab_keep.start()
-
-    @pl.loop(1, 32)
-    def _(step):
-        slab_send_copy(lax.rem(me + step, 32)).start()
 
     coeffs = coefficients(coeff_ref, index_ref)
     for halo in halos:
         halo.wait_recv()
 
+    slab_keep.start()
+
     @pl.loop(0, 32)
     def _(step):
+        @pl.when(step > 0)
+        def _():
+            slab_send_copy(lax.rem(me + step, 32)).start()
+
         rows = pl.ds(pl.multiple_of(step * 8, 8), 8)
         for r in range(4):
             light_ref[r, rows, :] = lighting(field_ref[r, rows, :], halo_ref[0, rows, :], halo_ref[1, rows, :], r)
@@ -287,10 +318,10 @@
 
     zero = jnp.zeros((8, 128), f32)
     c0, c1, c2, _, depth_sum = lax.fori_loop(0, 32, body, (zero, zero, zero, zero + 1.0, zero))
-    image_out[0] = c0
-    image_out[1] = c1
-    image_out[2] = c2
-    image_out[3] = jnp.exp(depth_sum * -tau_scale)
+    for channel, image in enumerate((c0, c1, c2, jnp.exp(depth_sum * -tau_scale))):
+        for y in range(4):
+            moved = pltpu.roll(image, 128 - 32 * y, 1) if y else image
+            image_out[pl.ds(channel * 4 + y, 8, stride=16), :] = moved
 
     slab_keep.wait()
 
@@ -322,15 +353,16 @@
     sem = pltpu.SemaphoreType.DMA
     field, image = pl.pallas_call(
         kernel,
-        out_shape=[jax.ShapeDtypeStruct((1024, 128), f32), jax.ShapeDtypeStruct((4, 8, 128), f32)],
+        out_shape=[jax.ShapeDtypeStruct((1024, 128), f32), jax.ShapeDtypeStruct((128, 128), f32)],
         in_specs=[smem, smem, vmem, hbm, hbm],
         out_specs=[vmem, vmem],
         scratch_shapes=[
+            pltpu.VMEM((256, NX), bf16),
             pltpu.VMEM((8, 2, NX, 256), bf16),
             pltpu.VMEM((4, 512, 512), bf16),
             pltpu.VMEM((2, 128, 128), f32),
-            pltpu.VMEM((32, 2, 32, 128), f32),
-            pltpu.VMEM((32, 2, 32, 128), f32),
+            pltpu.VMEM((32, 80, 128), jnp.int16),
+            pltpu.VMEM((32, 80, 128), jnp.int16),
             pltpu.VMEM((4, 512, 256), bf16),
             pltpu.VMEM((4, 256, 128), f32),
             pltpu.VMEM((4, 256, 128), f32),
@@ -340,11 +372,11 @@
             sem((8,)), sem, sem((32,)), sem((32,)), sem((2,)), sem((2,)), sem((32,)), sem((32,)),
         ],
         compiler_params=pltpu.CompilerParams(
-            collective_id=0, has_side_effects=True, vmem_limit_bytes=40 * 2**20
+            collective_id=0, has_side_effects=True, vmem_limit_bytes=60 * 2**20
         ),
-    )(transfer_coeffs.reshape(8, 16), transfer_index, spectrum.reshape(256, NX), x_tab, z_tab)
+    )(transfer_coeffs.transpose(1, 2, 0), transfer_index, spectrum, x_tab, z_tab)
     scalar_field = field.reshape(32, 8, 4, 128).transpose(0, 2, 1, 3).reshape(32, 4, NX)
-    rendered = jnp.transpose(image.reshape(4, 8, 4, 32), (1, 0, 2, 3))
+    rendered = image[:, :32].reshape(8, 4, 4, 32)
     return scalar_field, rendered
 
 

time: 65.2 us -> 54.7 us (0.84); the launches traced: 64.2 us -> 54.4 us
  local copies, waits for them, and re-layouts: 9.08 us -> 3.34 us
  Pallas kernels: 54.4 us -> 50.4 us
    pallas_call x1, Pallas kernels: 54.4 us -> 50.4 us  [body(): pl.pallas_call(kernel, out_shape=[jax.ShapeDtypeStruct((1024, 128), f32),...]
    unnamed x7 -> x2, local copies, waits for them, and re-layouts: 6.42 us -> 3.34 us
    reshape x4 -> x0, local copies, waits for them, and re-layouts: 2.66 us -> none  [the longest x1 1.16 us: body(): spectrum.reshape(256, NX)]
where the time goes in v2:
time: 54.7 us; the launch traced here: 54.4 us
  Pallas kernels  50.4 us (92%)
  local copies, waits for them, and re-layouts  3.34 us (6%)
  between operations  0.64 us (1%)
    pallas_call x1, Pallas kernels, body(): pl.pallas_call(kernel, out_shape=[jax.ShapeDtypeStruct((1024, 128), f32),...  50.4 us
    unnamed x2, local copies, waits for them, and re-layouts  3.34 us

profile of v2, /device:TPU:1, one launch (start us, length us, event | category | flops | bytes accessed | tf_op | source)
XLA Modules:
  0.0 54.4 jit_solution(8077914040903069393)
XLA Ops:
  0.6 50.4 %shard_map.68 = (f32[1024,128]{1,0:T(8,128)}, f32[128,128]{1,0:T(8,128)}) custom-call(f32[4,4,8]{2,1,0:T(4,128)} %bitcast.10, s32[8]{0:T(128)} %index_ref.1, bf16[2,32,4,1024]{3,2,1,0:T(4,128)(2,1)} %spectrum_ref.1, bf16[8,2,1024,256]{3,2,1,0:T(8,128)(2,1)} %constant.4.clone.x_hbm, bf16[4,512,512]{2,1,0:T(8,128)(2,1)} %constant.5.clone.z_hbm), custom_call_target="tpu_custom_call" | custom-call | tf_op jit(solution)/shard_map/pallas_call | solution.py:354
  51.1 1.9 %copy.10 = f32[32,4,1024]{2,1,0:T(4,128)} copy(f32[32,4,1024]{2,1,0:T(4,128)} %bitcast.8) | data formatting | bytes 1048576
  53.0 1.5 %copy.11 = f32[8,4,4,32]{3,2,1,0:T(4,128)} copy(f32[8,4,4,32]{3,2,1,0:T(4,128)} %bitcast.9) | data formatting | bytes 32768

commit v3 on v2

--- a/solution.py
+++ b/solution.py
@@ -14,7 +14,6 @@
 density = 2.0
 shade_gain = 0.4
 tau_scale = density / NZ
-LN2 = math.log(2.0)
 f32 = jnp.float32
 bf16 = jnp.bfloat16
 MESH = pl.DeviceIdType.MESH
@@ -27,10 +26,10 @@
 
 
 def x_table():
-    index = np.arange(NX)
-    angles = (index[:, None] * index[None, :] % NX) * (2.0 * np.pi / NX)
-    tables = [split_table(t / math.sqrt(NX)).reshape(2, NX, 8, 128) for t in (np.cos(angles), np.sin(angles))]
-    return np.ascontiguousarray(np.concatenate(tables, axis=3).transpose(2, 0, 1, 3))
+    k = 4 * np.arange(256)[None, :, None] + np.arange(4)[:, None, None]
+    angles = (k * np.arange(256)[None, None, :] % NX) * (2.0 * np.pi / NX)
+    tables = [split_table(t / math.sqrt(NX)).reshape(2, 4, 256, 2, 128) for t in (np.cos(angles), np.sin(angles))]
+    return np.ascontiguousarray(np.concatenate(tables, axis=4).transpose(3, 0, 1, 2, 4))
 
 
 def z_table():
@@ -87,18 +86,28 @@
 def encode(parts):
     peak = jnp.maximum(jnp.abs(parts[0]), jnp.abs(parts[1]))
     peak = jnp.maximum(jnp.max(peak, axis=0, keepdims=True), 1e-30)
-    level = jnp.floor(jnp.log(peak) * (256.0 / LN2)) + 2.0
-    level = jnp.broadcast_to(level, (16, 128))
-    scale = jnp.exp2(level[:8] * (-1.0 / 256.0)) * 32766.0
-    scale = jnp.concatenate([scale] * 4)
-    codes = [jnp.round(part * scale).astype(jnp.int32).astype(jnp.int16) for part in parts]
-    return codes, level.astype(jnp.int32).astype(jnp.int16)
-
-
-def decode(codes, level):
-    step = jnp.exp2(level.astype(jnp.int32).astype(f32)[:8] * (1.0 / 256.0)) * (1.0 / 32766.0)
-    step = jnp.concatenate([step] * 4)
+    codes = [jnp.round(part * (32766.0 / peak)).astype(jnp.int32).astype(jnp.int16) for part in parts]
+    return codes, peak * (1.0 / 32766.0)
+
+
+def decode(codes, step):
     return [code.astype(jnp.int32).astype(f32) * step for code in codes]
+
+
+def gather_classes(rows_ref, class_ref):
+    source = lax.broadcasted_iota(jnp.int32, (256, 256), 0)
+    target = lax.broadcasted_iota(jnp.int32, (256, 256), 1)
+    move = jnp.where(source == 4 * (target % 64) + target // 64, 1.0, 0.0).astype(bf16)
+    low_half = lax.broadcasted_iota(jnp.int32, (256, 128), 1) < 64
+    for half in range(2):
+        p = [dot(rows_ref[:, 512 * half + 256 * t : 512 * half + 256 * (t + 1)], move) for t in range(2)]
+        for j in range(4):
+            a, b = (q[:, 128 * (j // 2) : 128 * (j // 2 + 1)] for q in p)
+            if j % 2 == 0:
+                value = jnp.where(low_half, a, pltpu.roll(b, 64, 1))
+            else:
+                value = jnp.where(low_half, pltpu.roll(a, 64, 1), b)
+            class_ref[j, :, 128 * half : 128 * (half + 1)] = value.astype(bf16)
 
 
 def softplus(coeffs, s):
@@ -138,7 +147,7 @@
 def kernel(
     coeff_ref, index_ref, spectrum_ref, x_hbm, z_hbm,
     field_out, image_out,
-    row_ref, x_ref, z_ref, mode_ref, send_ref, recv_ref, pair_ref, field_ref, light_ref, pack_ref, halo_ref, slab_ref,
+    row_ref, class_ref, x_ref, z_ref, wave_ref, mode_ref, send_ref, recv_ref, step_out, step_in, pair_ref, value_ref, glow_ref, field_ref, light_ref, pack_ref, halo_ref, slab_ref,
     x_sem, z_sem, send_sem, recv_sem, halo_send, halo_recv, slab_send, slab_recv,
 ):
     me = lax.axis_index("depth")
@@ -147,17 +156,16 @@
     next_plane = lax.rem(plane + 1, planes)
     last_plane = lax.rem(plane + planes - 1, planes)
 
-    def chunk_of(step):
-        return lax.rem(me // 4 + step, 8)
+    def half_of(step):
+        return lax.rem(me // 4 + step, 2)
 
     def x_copy(step):
-        chunk = chunk_of(step)
-        return pltpu.make_async_copy(x_hbm.at[chunk], x_ref.at[chunk], x_sem.at[step])
+        half = half_of(step)
+        return pltpu.make_async_copy(x_hbm.at[half], x_ref.at[half], x_sem.at[step])
 
     z_copy = pltpu.make_async_copy(z_hbm, z_ref, z_sem)
 
-    @pl.loop(0, 8)
-    def _(step):
+    for step in range(2):
         x_copy(step).start()
 
     z_copy.start()
@@ -171,57 +179,85 @@
     pl.semaphore_signal(barrier, inc=1, device_id={"plane": next_plane}, device_id_type=MESH)
     pl.semaphore_signal(barrier, inc=1, device_id={"plane": last_plane}, device_id_type=MESH)
 
-    def mode_send(to):
-        return pltpu.make_async_remote_copy(
-            src_ref=send_ref.at[to], dst_ref=recv_ref.at[me], send_sem=send_sem.at[to], recv_sem=recv_sem.at[me],
-            device_id={"depth": to}, device_id_type=MESH,
-        )
-
-    def mode_recv(source):
-        return pltpu.make_async_remote_copy(
-            src_ref=send_ref.at[source], dst_ref=recv_ref.at[source], send_sem=send_sem.at[source],
-            recv_sem=recv_sem.at[source], device_id={"depth": source}, device_id_type=MESH,
-        )
-
-    def mode_keep():
-        return pltpu.make_async_copy(send_ref.at[me], recv_ref.at[me], recv_sem.at[me])
+    def mode_sends(to):
+        return [
+            pltpu.make_async_remote_copy(
+                src_ref=out_ref.at[to], dst_ref=in_ref.at[me], send_sem=send_sem.at[k, to], recv_sem=recv_sem.at[k, me],
+                device_id={"depth": to}, device_id_type=MESH,
+            )
+            for k, (out_ref, in_ref) in enumerate(((send_ref, recv_ref), (step_out, step_in)))
+        ]
+
+    def mode_recvs(source):
+        return [
+            pltpu.make_async_remote_copy(
+                src_ref=out_ref.at[source], dst_ref=in_ref.at[source], send_sem=send_sem.at[k, source],
+                recv_sem=recv_sem.at[k, source], device_id={"depth": source}, device_id_type=MESH,
+            )
+            for k, (out_ref, in_ref) in enumerate(((send_ref, recv_ref), (step_out, step_in)))
+        ]
+
+    def mode_keeps():
+        return [
+            pltpu.make_async_copy(out_ref.at[me], in_ref.at[me], recv_sem.at[k, me])
+            for k, (out_ref, in_ref) in enumerate(((send_ref, recv_ref), (step_out, step_in)))
+        ]
 
     row_ref[...] = spectrum_ref[...].reshape(256, NX)
-
-    @pl.loop(0, 8)
-    def _(step):
-        chunk = chunk_of(step)
+    gather_classes(row_ref, class_ref)
+
+    @pl.loop(0, 2)
+    def _(step):
+        half = half_of(step)
         x_copy(step).wait()
-        modes = row_ref[...]
-        waves = dot(modes, x_ref[chunk, 0]) + dot(modes, x_ref[chunk, 1])
-        mode_ref[0] = waves[:128, :128] - waves[128:, 128:]
-        mode_ref[1] = waves[:128, 128:] + waves[128:, :128]
-        parts = [[] for _ in range(4)]
-        for part in range(2):
-            rows = [mode_ref[part, pl.ds(y, 32, stride=4), :] for y in range(4)]
-            for d in range(4):
-                parts[d].append(shuffle(rows, d))
-        for d in range(4):
-            codes, level = encode(parts[d])
-            send_ref[chunk * 4 + d, 0:32] = codes[0]
-            send_ref[chunk * 4 + d, 32:64] = codes[1]
-            send_ref[chunk * 4 + d, 64:80] = level
+        for j in range(4):
+            waves = dot(class_ref[j], x_ref[half, 0, j]) + dot(class_ref[j], x_ref[half, 1, j])
+            wave_ref[j, 0] = waves[:128, :128] - waves[128:, 128:]
+            wave_ref[j, 1] = waves[:128, 128:] + waves[128:, :128]
+        for k in range(4):
+            rows = slice(32 * k, 32 * k + 32)
+            re = [wave_ref[j, 0, rows] for j in range(4)]
+            im = [wave_ref[j, 1, rows] for j in range(4)]
+            for i, pair in enumerate(residues(re, im)):
+                mode_ref[i, 0, rows] = pair[0]
+                mode_ref[i, 1, rows] = pair[1]
 
         @pl.when(step == 0)
         def _():
             pl.semaphore_wait(barrier, 33)
 
         @pl.loop(0, 4)
-        def _(d):
-            to = chunk * 4 + d
-
-            @pl.when(to != me)
-            def _():
-                mode_send(to).start()
-
-            @pl.when(to == me)
-            def _():
-                mode_keep().start()
+        def _(turn):
+            i = lax.rem(me // 8 + turn + turn // 2 - 2 * (turn // 3), 4)
+            first = 8 * i + 4 * half
+            parts = [[] for _ in range(4)]
+            for part in range(2):
+                rows = [mode_ref[i, part, pl.ds(y, 32, stride=4), :] for y in range(4)]
+                for d in range(4):
+                    parts[d].append(shuffle(rows, d))
+            for d in range(4):
+                codes, size = encode(parts[d])
+                send_ref[first + d, 0:32] = codes[0]
+                send_ref[first + d, 32:64] = codes[1]
+                step_out[first + d] = size
+
+            @pl.loop(0, 4)
+            def _(d):
+                to = first + d
+
+                @pl.when(to != me)
+                def _():
+                    for copy in mode_sends(to):
+                        copy.start()
+
+                @pl.when(to == me)
+                def _():
+                    for copy in mode_keeps():
+                        copy.start()
+
+    coeffs = coefficients(coeff_ref, index_ref)
+    for n, value in enumerate(coeffs):
+        value_ref[n] = value
 
     @pl.loop(0, 8)
     def _(s):
@@ -231,16 +267,18 @@
 
             @pl.when(source != me)
             def _():
-                mode_recv(source).wait_recv()
+                for copy in mode_recvs(source):
+                    copy.wait_recv()
 
             @pl.when(source == me)
             def _():
-                mode_keep().wait()
+                for copy in mode_keeps():
+                    copy.wait()
 
         re, im = [], []
         for j in range(4):
             got = recv_ref.at[s + 8 * j]
-            real, imag = decode([got[0:32], got[32:64]], got[64:80])
+            real, imag = decode([got[0:32], got[32:64]], step_in[s + 8 * j])
             re.append(real)
             im.append(imag)
         for r, pair in enumerate(residues(re, im)):
@@ -257,9 +295,9 @@
         p = dot(z_ref[r], pair_ref[r])
         field_ref[r] = (p[:256, :128] + p[:256, 128:]) + (p[256:, :128] + p[256:, 128:])
 
-    @pl.loop(0, 32)
-    def _(step):
-        rows = pl.ds(pl.multiple_of(step * 8, 8), 8)
+    @pl.loop(0, 4)
+    def _(step):
+        rows = pl.ds(pl.multiple_of(step * 64, 64), 64)
         parts = [field_ref[r, rows, :] for r in range(4)]
         pack_ref[0, rows, :] = shuffle(parts, 3)
         pack_ref[1, rows, :] = shuffle(parts, 0)
@@ -291,33 +329,63 @@
 
     slab_keep = pltpu.make_async_copy(own_rows(me), slab_ref.at[me], slab_recv.at[me])
 
-    coeffs = coefficients(coeff_ref, index_ref)
+    slab_keep.start()
+    coeffs = [value_ref[n] for n in range(16)]
+
+    def cell_row(ref, step, r, k):
+        rows = pl.ds(pl.multiple_of(step * 8, 8), 8)
+        return jnp.broadcast_to(ref[r, rows, :][k : k + 1, :], (8, 128))
+
+    def front(step, state):
+        @pl.loop(0, 2)
+        def _(n):
+            @pl.when(2 * step + n > 0)
+            def _():
+                slab_send_copy(lax.rem(me + 2 * step + n, 32)).start()
+
+        through, depth_sum = state
+        for k in range(8):
+            for r in range(4):
+                s = cell_row(field_ref, step, r, k)
+                depth = softplus(coeffs[12:16], s)
+                weight = through * opacity(depth)
+                through = through - weight
+                depth_sum = depth_sum + depth
+                for j in range(3):
+                    glow_ref[step, 4 * k + r, j] = weight * softplus(coeffs[4 * j : 4 * j + 4], s)
+        return through, depth_sum
+
+    zero = jnp.zeros((8, 128), f32)
+    through, depth_sum = lax.fori_loop(0, 16, front, (zero + 1.0, zero))
+
     for halo in halos:
         halo.wait_recv()
 
-    slab_keep.start()
-
-    @pl.loop(0, 32)
-    def _(step):
-        @pl.when(step > 0)
-        def _():
-            slab_send_copy(lax.rem(me + step, 32)).start()
-
-        rows = pl.ds(pl.multiple_of(step * 8, 8), 8)
+    @pl.loop(0, 8)
+    def _(step):
+        rows = pl.ds(pl.multiple_of(step * 32, 32), 32)
         for r in range(4):
             light_ref[r, rows, :] = lighting(field_ref[r, rows, :], halo_ref[0, rows, :], halo_ref[1, rows, :], r)
 
-    def body(step, state):
-        rows = pl.ds(pl.multiple_of(step * 8, 8), 8)
+    def lit(step, colors):
+        colors = list(colors)
         for k in range(8):
             for r in range(4):
-                s = jnp.broadcast_to(field_ref[r, rows, :][k : k + 1, :], (8, 128))
-                light = jnp.broadcast_to(light_ref[r, rows, :][k : k + 1, :], (8, 128))
-                state = render_step(coeffs, s, light, state)
+                light = cell_row(light_ref, step, r, k)
+                for j in range(3):
+                    colors[j] = colors[j] + light * glow_ref[step, 4 * k + r, j]
+        return tuple(colors)
+
+    colors = lax.fori_loop(0, 16, lit, (zero, zero, zero))
+
+    def body(step, state):
+        for k in range(8):
+            for r in range(4):
+                s = cell_row(field_ref, step, r, k)
+                state = render_step(coeffs, s, cell_row(light_ref, step, r, k), state)
         return state
 
-    zero = jnp.zeros((8, 128), f32)
-    c0, c1, c2, _, depth_sum = lax.fori_loop(0, 32, body, (zero, zero, zero, zero + 1.0, zero))
+    c0, c1, c2, _, depth_sum = lax.fori_loop(16, 32, body, (*colors, through, depth_sum))
     for channel, image in enumerate((c0, c1, c2, jnp.exp(depth_sum * -tau_scale))):
         for y in range(4):
             moved = pltpu.roll(image, 128 - 32 * y, 1) if y else image
@@ -339,7 +407,8 @@
     @pl.loop(1, 32)
     def _(step):
         to = lax.rem(me + step, 32)
-        mode_send(to).wait_send()
+        for copy in mode_sends(to):
+            copy.wait_send()
         slab_send_copy(to).wait_send()
 
     for halo in halos:
@@ -358,18 +427,24 @@
         out_specs=[vmem, vmem],
         scratch_shapes=[
             pltpu.VMEM((256, NX), bf16),
-            pltpu.VMEM((8, 2, NX, 256), bf16),
+            pltpu.VMEM((4, 256, 256), bf16),
+            pltpu.VMEM((2, 2, 4, 256, 256), bf16),
             pltpu.VMEM((4, 512, 512), bf16),
-            pltpu.VMEM((2, 128, 128), f32),
-            pltpu.VMEM((32, 80, 128), jnp.int16),
-            pltpu.VMEM((32, 80, 128), jnp.int16),
+            pltpu.VMEM((4, 2, 128, 128), f32),
+            pltpu.VMEM((4, 2, 128, 128), f32),
+            pltpu.VMEM((32, 64, 128), jnp.int16),
+            pltpu.VMEM((32, 64, 128), jnp.int16),
+            pltpu.VMEM((32, 1, 128), f32),
+            pltpu.VMEM((32, 1, 128), f32),
             pltpu.VMEM((4, 512, 256), bf16),
+            pltpu.VMEM((16, 8, 128), f32),
+            pltpu.VMEM((16, 32, 3, 8, 128), f32),
             pltpu.VMEM((4, 256, 128), f32),
             pltpu.VMEM((4, 256, 128), f32),
             pltpu.VMEM((2, 256, 128), f32),
             pltpu.VMEM((2, 256, 128), f32),
             pltpu.VMEM((32, 4, 8, 128), f32),
-            sem((8,)), sem, sem((32,)), sem((32,)), sem((2,)), sem((2,)), sem((32,)), sem((32,)),
+            sem((2,)), sem, sem((2, 32)), sem((2, 32)), sem((2,)), sem((2,)), sem((32,)), sem((32,)),
         ],
         compiler_params=pltpu.CompilerParams(
             collective_id=0, has_side_effects=True, vmem_limit_bytes=60 * 2**20

time: 54.7 us -> 44.7 us (0.82)
  Pallas kernels: 50.4 us -> 40.5 us
    pallas_call x1, Pallas kernels: 50.4 us -> 40.5 us  [body(): pl.pallas_call(kernel, out_shape=[jax.ShapeDtypeStruct((1024, 128), f32),...]
where the time goes in v3:
time: 44.7 us; the launch traced here: 44.5 us
  Pallas kernels  40.5 us (91%)
  local copies, waits for them, and re-layouts  3.34 us (7%)
  between operations  0.64 us (1%)
    pallas_call x1, Pallas kernels, body(): pl.pallas_call(kernel, out_shape=[jax.ShapeDtypeStruct((1024, 128), f32),...  40.5 us
    unnamed x2, local copies, waits for them, and re-layouts  3.34 us

profile of v3, /device:TPU:1, one launch (start us, length us, event | category | flops | bytes accessed | tf_op | source)
XLA Modules:
  0.0 44.5 jit_solution(17943289190142098638)
XLA Ops:
  0.6 40.5 %shard_map.68 = (f32[1024,128]{1,0:T(8,128)}, f32[128,128]{1,0:T(8,128)}) custom-call(f32[4,4,8]{2,1,0:T(4,128)} %bitcast.10, s32[8]{0:T(128)} %index_ref.1, bf16[2,32,4,1024]{3,2,1,0:T(4,128)(2,1)} %spectrum_ref.1, bf16[2,2,4,256,256]{4,3,2,1,0:T(8,128)(2,1)} %constant.4.clone.x_hbm, bf16[4,512,512]{2,1,0:T(8,128)(2,1)} %constant.5.clone.z_hbm), custom_call_target="tpu_custom_call" | custom-call | tf_op jit(solution)/shard_map/pallas_call | solution.py:423
  41.2 1.9 %copy.10 = f32[32,4,1024]{2,1,0:T(4,128)} copy(f32[32,4,1024]{2,1,0:T(4,128)} %bitcast.8) | data formatting | bytes 1048576
  43.0 1.5 %copy.11 = f32[8,4,4,32]{3,2,1,0:T(4,128)} copy(f32[8,4,4,32]{3,2,1,0:T(4,128)} %bitcast.9) | data formatting | bytes 32768

commit v4 on v3

--- a/solution.py
+++ b/solution.py
@@ -86,12 +86,15 @@
 def encode(parts):
     peak = jnp.maximum(jnp.abs(parts[0]), jnp.abs(parts[1]))
     peak = jnp.maximum(jnp.max(peak, axis=0, keepdims=True), 1e-30)
-    codes = [jnp.round(part * (32766.0 / peak)).astype(jnp.int32).astype(jnp.int16) for part in parts]
-    return codes, peak * (1.0 / 32766.0)
-
-
-def decode(codes, step):
-    return [code.astype(jnp.int32).astype(f32) * step for code in codes]
+    level = jnp.floor(jnp.log(peak) * (256.0 / math.log(2.0))) + 2.0
+    scale = jnp.exp2(level * (-1.0 / 256.0)) * 32766.0
+    re, im = (jnp.round(part * scale).astype(jnp.int32) for part in parts)
+    return (re << 16) | (im & 0xFFFF), level.astype(jnp.int32)
+
+
+def decode(codes, level):
+    step = jnp.exp2(level.astype(f32) * (1.0 / 256.0)) * (1.0 / 32766.0)
+    return (codes >> 16).astype(f32) * step, ((codes << 16) >> 16).astype(f32) * step
 
 
 def gather_classes(rows_ref, class_ref):
@@ -110,28 +113,59 @@
             class_ref[j, :, 128 * half : 128 * (half + 1)] = value.astype(bf16)
 
 
-def softplus(coeffs, s):
-    p = ((coeffs[3] * s + coeffs[2]) * s + coeffs[1]) * s + coeffs[0]
+def softplus(p):
     return jnp.maximum(p, jnp.log(1.0 + jnp.exp(jnp.minimum(p, 80.0))))
 
 
 def opacity(depth):
     k1, k2, k3 = tau_scale, tau_scale**2 / 2, tau_scale**3 / 6
     small = depth * (k1 - depth * (k2 - depth * k3))
-    large = 1.0 - jnp.exp(depth * -tau_scale)
+    large = 1.0 - jnp.exp2(depth * (-tau_scale / math.log(2.0)))
     return jnp.where(depth < 16.0, small, large)
 
 
-def render_step(coeffs, s, light, state):
-    c0, c1, c2, through, depth_sum = state
-    depth = softplus(coeffs[12:16], s)
-    weight = through * opacity(depth)
-    through = through - weight
-    weight = weight * light
-    c0 = c0 + weight * softplus(coeffs[0:4], s)
-    c1 = c1 + weight * softplus(coeffs[4:8], s)
-    c2 = c2 + weight * softplus(coeffs[8:12], s)
-    return c0, c1, c2, through, depth_sum + depth
+def pieces(value, count):
+    result = []
+    for _ in range(count):
+        high = value.astype(bf16)
+        result.append(high)
+        value = value - high.astype(f32)
+    return result
+
+
+def fill_polynomials(coeffs, poly_ref):
+    lane = lax.broadcasted_iota(jnp.int32, (8, 128), 1)
+    tables = []
+    for channel in range(4):
+        terms = []
+        for n in (1, 2, 3):
+            high, low = (piece.astype(f32) for piece in pieces(coeffs[4 * channel + n], 2))
+            terms += [high, high, low, low]
+        terms += [piece.astype(f32) for piece in pieces(coeffs[4 * channel], 3)] + [jnp.zeros((8, 128), f32)]
+        for tile in range(2):
+            value = terms[8 * tile]
+            for t in range(1, 8):
+                value = jnp.where(lane // 16 == t, terms[8 * tile + t], value)
+            tables.append(value)
+
+    @pl.loop(0, 16)
+    def _(cell):
+        here = lane % 16 == cell
+        for pair in range(2):
+            rows = pl.ds(pl.multiple_of(cell * 32 + pair * 16, 16), 16)
+            for tile in range(2):
+                both = [jnp.where(here, tables[2 * (2 * pair + c) + tile], 0.0) for c in range(2)]
+                poly_ref[rows, 128 * tile : 128 * (tile + 1)] = jnp.concatenate(both).astype(bf16)
+
+
+def powers(s):
+    result = []
+    power = s
+    for n in range(3):
+        high, low = pieces(power, 2)
+        result += [high, low, high, low]
+        power = power * s
+    return jnp.concatenate(result + [jnp.ones((64, 128), bf16)])
 
 
 def shuffle(parts, place):
@@ -147,7 +181,7 @@
 def kernel(
     coeff_ref, index_ref, spectrum_ref, x_hbm, z_hbm,
     field_out, image_out,
-    row_ref, class_ref, x_ref, z_ref, wave_ref, mode_ref, send_ref, recv_ref, step_out, step_in, pair_ref, value_ref, glow_ref, field_ref, light_ref, pack_ref, halo_ref, slab_ref,
+    row_ref, class_ref, x_ref, z_ref, wave_ref, mode_ref, send_ref, recv_ref, pair_ref, poly_ref, even_ref, odd_ref, glow_ref, field_ref, light_ref, pack_ref, halo_ref, slab_ref,
     x_sem, z_sem, send_sem, recv_sem, halo_send, halo_recv, slab_send, slab_recv,
 ):
     me = lax.axis_index("depth")
@@ -179,29 +213,20 @@
     pl.semaphore_signal(barrier, inc=1, device_id={"plane": next_plane}, device_id_type=MESH)
     pl.semaphore_signal(barrier, inc=1, device_id={"plane": last_plane}, device_id_type=MESH)
 
-    def mode_sends(to):
-        return [
-            pltpu.make_async_remote_copy(
-                src_ref=out_ref.at[to], dst_ref=in_ref.at[me], send_sem=send_sem.at[k, to], recv_sem=recv_sem.at[k, me],
-                device_id={"depth": to}, device_id_type=MESH,
-            )
-            for k, (out_ref, in_ref) in enumerate(((send_ref, recv_ref), (step_out, step_in)))
-        ]
-
-    def mode_recvs(source):
-        return [
-            pltpu.make_async_remote_copy(
-                src_ref=out_ref.at[source], dst_ref=in_ref.at[source], send_sem=send_sem.at[k, source],
-                recv_sem=recv_sem.at[k, source], device_id={"depth": source}, device_id_type=MESH,
-            )
-            for k, (out_ref, in_ref) in enumerate(((send_ref, recv_ref), (step_out, step_in)))
-        ]
-
-    def mode_keeps():
-        return [
-            pltpu.make_async_copy(out_ref.at[me], in_ref.at[me], recv_sem.at[k, me])
-            for k, (out_ref, in_ref) in enumerate(((send_ref, recv_ref), (step_out, step_in)))
-        ]
+    def mode_send(to):
+        return pltpu.make_async_remote_copy(
+            src_ref=send_ref.at[to], dst_ref=recv_ref.at[me], send_sem=send_sem.at[to], recv_sem=recv_sem.at[me],
+            device_id={"depth": to}, device_id_type=MESH,
+        )
+
+    def mode_recv(source):
+        return pltpu.make_async_remote_copy(
+            src_ref=send_ref.at[source], dst_ref=recv_ref.at[source], send_sem=send_sem.at[source],
+            recv_sem=recv_sem.at[source], device_id={"depth": source}, device_id_type=MESH,
+        )
+
+    def mode_keep():
+        return pltpu.make_async_copy(send_ref.at[me], recv_ref.at[me], recv_sem.at[me])
 
     row_ref[...] = spectrum_ref[...].reshape(256, NX)
     gather_classes(row_ref, class_ref)
@@ -236,10 +261,9 @@
                 for d in range(4):
                     parts[d].append(shuffle(rows, d))
             for d in range(4):
-                codes, size = encode(parts[d])
-                send_ref[first + d, 0:32] = codes[0]
-                send_ref[first + d, 32:64] = codes[1]
-                step_out[first + d] = size
+                codes, level = encode(parts[d])
+                send_ref[first + d, 0:32] = codes
+                send_ref[first + d, 32:33] = level
 
             @pl.loop(0, 4)
             def _(d):
@@ -247,17 +271,13 @@
 
                 @pl.when(to != me)
                 def _():
-                    for copy in mode_sends(to):
-                        copy.start()
+                    mode_send(to).start()
 
                 @pl.when(to == me)
                 def _():
-                    for copy in mode_keeps():
-                        copy.start()
-
-    coeffs = coefficients(coeff_ref, index_ref)
-    for n, value in enumerate(coeffs):
-        value_ref[n] = value
+                    mode_keep().start()
+
+    fill_polynomials(coefficients(coeff_ref, index_ref), poly_ref)
 
     @pl.loop(0, 8)
     def _(s):
@@ -267,18 +287,15 @@
 
             @pl.when(source != me)
             def _():
-                for copy in mode_recvs(source):
-                    copy.wait_recv()
+                mode_recv(source).wait_recv()
 
             @pl.when(source == me)
             def _():
-                for copy in mode_keeps():
-                    copy.wait()
+                mode_keep().wait()
 
         re, im = [], []
         for j in range(4):
-            got = recv_ref.at[s + 8 * j]
-            real, imag = decode([got[0:32], got[32:64]], step_in[s + 8 * j])
+            real, imag = decode(recv_ref[s + 8 * j, 0:32], recv_ref[s + 8 * j, 32:33])
             re.append(real)
             im.append(imag)
         for r, pair in enumerate(residues(re, im)):
@@ -330,33 +347,55 @@
     slab_keep = pltpu.make_async_copy(own_rows(me), slab_ref.at[me], slab_recv.at[me])
 
     slab_keep.start()
-    coeffs = [value_ref[n] for n in range(16)]
-
-    def cell_row(ref, step, r, k):
-        rows = pl.ds(pl.multiple_of(step * 8, 8), 8)
-        return jnp.broadcast_to(ref[r, rows, :][k : k + 1, :], (8, 128))
-
-    def front(step, state):
-        @pl.loop(0, 2)
-        def _(n):
-            @pl.when(2 * step + n > 0)
-            def _():
-                slab_send_copy(lax.rem(me + 2 * step + n, 32)).start()
-
+
+    def evaluate(block, to_ref):
+        rows = pl.ds(pl.multiple_of(jnp.minimum(block, 15) * 16, 16), 16)
+        for pair in range(2):
+            factors = [powers(field_ref[2 * pair + c, rows, :]) for c in range(2)]
+            to_ref[pair] = dot(poly_ref[...], jnp.concatenate(factors, axis=1))
+
+    def cell_depths(from_ref, r, k, channel):
+        first = 32 * k + 8 * channel
+        return softplus(from_ref[r // 2, first : first + 8, 128 * (r % 2) : 128 * (r % 2) + 128])
+
+    def cell_light(block, r, k):
+        rows = pl.ds(pl.multiple_of(block * 16, 16), 16)
+        return jnp.broadcast_to(light_ref[r, rows, :][k : k + 1, :], (8, 128))
+
+    def absorb(from_ref, r, k, through, depth_sum):
+        depth = cell_depths(from_ref, r, k, 3)
+        weight = through * opacity(depth)
+        return weight, through - weight, depth_sum + depth
+
+    def in_pairs(start, cells, slabs):
+        def step(n, state):
+            block = start + 2 * n
+            if slabs:
+                @pl.loop(0, 8)
+                def _(k):
+                    @pl.when(4 * block + k > 0)
+                    def _():
+                        slab_send_copy(lax.rem(me + 4 * block + k, 32)).start()
+
+            evaluate(block + 1, odd_ref)
+            state = cells(block, even_ref, state)
+            evaluate(block + 2, even_ref)
+            return cells(block + 1, odd_ref, state)
+
+        return step
+
+    def front(block, from_ref, state):
         through, depth_sum = state
-        for k in range(8):
+        for k in range(16):
             for r in range(4):
-                s = cell_row(field_ref, step, r, k)
-                depth = softplus(coeffs[12:16], s)
-                weight = through * opacity(depth)
-                through = through - weight
-                depth_sum = depth_sum + depth
+                weight, through, depth_sum = absorb(from_ref, r, k, through, depth_sum)
                 for j in range(3):
-                    glow_ref[step, 4 * k + r, j] = weight * softplus(coeffs[4 * j : 4 * j + 4], s)
+                    glow_ref[block, 4 * k + r, j] = weight * cell_depths(from_ref, r, k, j)
         return through, depth_sum
 
     zero = jnp.zeros((8, 128), f32)
-    through, depth_sum = lax.fori_loop(0, 16, front, (zero + 1.0, zero))
+    evaluate(0, even_ref)
+    through, depth_sum = lax.fori_loop(0, 4, in_pairs(0, front, True), (zero + 1.0, zero))
 
     for halo in halos:
         halo.wait_recv()
@@ -367,25 +406,28 @@
         for r in range(4):
             light_ref[r, rows, :] = lighting(field_ref[r, rows, :], halo_ref[0, rows, :], halo_ref[1, rows, :], r)
 
-    def lit(step, colors):
+    def lit(block, colors):
         colors = list(colors)
-        for k in range(8):
+        for k in range(16):
             for r in range(4):
-                light = cell_row(light_ref, step, r, k)
+                light = cell_light(block, r, k)
                 for j in range(3):
-                    colors[j] = colors[j] + light * glow_ref[step, 4 * k + r, j]
+                    colors[j] = colors[j] + light * glow_ref[block, 4 * k + r, j]
         return tuple(colors)
 
-    colors = lax.fori_loop(0, 16, lit, (zero, zero, zero))
-
-    def body(step, state):
-        for k in range(8):
+    colors = lax.fori_loop(0, 8, lit, (zero, zero, zero))
+
+    def back(block, from_ref, state):
+        *colors, through, depth_sum = state
+        for k in range(16):
             for r in range(4):
-                s = cell_row(field_ref, step, r, k)
-                state = render_step(coeffs, s, cell_row(light_ref, step, r, k), state)
-        return state
-
-    c0, c1, c2, _, depth_sum = lax.fori_loop(16, 32, body, (*colors, through, depth_sum))
+                weight, through, depth_sum = absorb(from_ref, r, k, through, depth_sum)
+                weight = weight * cell_light(block, r, k)
+                for j in range(3):
+                    colors[j] = colors[j] + weight * cell_depths(from_ref, r, k, j)
+        return (*colors, through, depth_sum)
+
+    c0, c1, c2, _, depth_sum = lax.fori_loop(0, 4, in_pairs(8, back, False), (*colors, through, depth_sum))
     for channel, image in enumerate((c0, c1, c2, jnp.exp(depth_sum * -tau_scale))):
         for y in range(4):
             moved = pltpu.roll(image, 128 - 32 * y, 1) if y else image
@@ -407,8 +449,7 @@
     @pl.loop(1, 32)
     def _(step):
         to = lax.rem(me + step, 32)
-        for copy in mode_sends(to):
-            copy.wait_send()
+        mode_send(to).wait_send()
         slab_send_copy(to).wait_send()
 
     for halo in halos:
@@ -432,19 +473,19 @@
             pltpu.VMEM((4, 512, 512), bf16),
             pltpu.VMEM((4, 2, 128, 128), f32),
             pltpu.VMEM((4, 2, 128, 128), f32),
-            pltpu.VMEM((32, 64, 128), jnp.int16),
-            pltpu.VMEM((32, 64, 128), jnp.int16),
-            pltpu.VMEM((32, 1, 128), f32),
-            pltpu.VMEM((32, 1, 128), f32),
+            pltpu.VMEM((32, 33, 128), jnp.int32),
+            pltpu.VMEM((32, 33, 128), jnp.int32),
             pltpu.VMEM((4, 512, 256), bf16),
-            pltpu.VMEM((16, 8, 128), f32),
-            pltpu.VMEM((16, 32, 3, 8, 128), f32),
+            pltpu.VMEM((512, 256), bf16),
+            pltpu.VMEM((2, 512, 256), f32),
+            pltpu.VMEM((2, 512, 256), f32),
+            pltpu.VMEM((8, 64, 3, 8, 128), f32),
             pltpu.VMEM((4, 256, 128), f32),
             pltpu.VMEM((4, 256, 128), f32),
             pltpu.VMEM((2, 256, 128), f32),
             pltpu.VMEM((2, 256, 128), f32),
             pltpu.VMEM((32, 4, 8, 128), f32),
-            sem((2,)), sem, sem((2, 32)), sem((2, 32)), sem((2,)), sem((2,)), sem((32,)), sem((32,)),
+            sem((2,)), sem, sem((32,)), sem((32,)), sem((2,)), sem((2,)), sem((32,)), sem((32,)),
         ],
         compiler_params=pltpu.CompilerParams(
             collective_id=0, has_side_effects=True, vmem_limit_bytes=60 * 2**20

time: 44.7 us -> 43.8 us (0.980)
  Pallas kernels: 40.5 us -> 39.6 us
    pallas_call x1, Pallas kernels: 40.5 us -> 39.6 us  [body(): pl.pallas_call(kernel, out_shape=[jax.ShapeDtypeStruct((1024, 128), f32),...]
where the time goes in v4:
time: 43.8 us; the launch traced here: 43.6 us
  Pallas kernels  39.6 us (90%)
  local copies, waits for them, and re-layouts  3.34 us (8%)
  between operations  0.64 us (1%)
    pallas_call x1, Pallas kernels, body(): pl.pallas_call(kernel, out_shape=[jax.ShapeDtypeStruct((1024, 128), f32),...  39.6 us
    unnamed x2, local copies, waits for them, and re-layouts  3.34 us

profile of v4, /device:TPU:1, one launch (start us, length us, event | category | flops | bytes accessed | tf_op | source)
XLA Modules:
  0.0 43.6 jit_solution(4662461872794238270)
XLA Ops:
  0.6 39.6 %shard_map.68 = (f32[1024,128]{1,0:T(8,128)}, f32[128,128]{1,0:T(8,128)}) custom-call(f32[4,4,8]{2,1,0:T(4,128)} %bitcast.10, s32[8]{0:T(128)} %index_ref.1, bf16[2,32,4,1024]{3,2,1,0:T(4,128)(2,1)} %spectrum_ref.1, bf16[2,2,4,256,256]{4,3,2,1,0:T(8,128)(2,1)} %constant.4.clone.x_hbm, bf16[4,512,512]{2,1,0:T(8,128)(2,1)} %constant.5.clone.z_hbm), custom_call_target="tpu_custom_call" | custom-call | tf_op jit(solution)/shard_map/pallas_call | solution.py:464
  40.2 1.9 %copy.10 = f32[32,4,1024]{2,1,0:T(4,128)} copy(f32[32,4,1024]{2,1,0:T(4,128)} %bitcast.8) | data formatting | bytes 1048576
  42.1 1.5 %copy.11 = f32[8,4,4,32]{3,2,1,0:T(4,128)} copy(f32[8,4,4,32]{3,2,1,0:T(4,128)} %bitcast.9) | data formatting | bytes 32768

commit v5 on v4

--- a/solution.py
+++ b/solution.py
@@ -179,10 +179,10 @@
 
 
 def kernel(
-    coeff_ref, index_ref, spectrum_ref, x_hbm, z_hbm,
+    coeff_hbm, index_hbm, spectrum_hbm, x_hbm, z_hbm,
     field_out, image_out,
-    row_ref, class_ref, x_ref, z_ref, wave_ref, mode_ref, send_ref, recv_ref, pair_ref, poly_ref, even_ref, odd_ref, glow_ref, field_ref, light_ref, pack_ref, halo_ref, slab_ref,
-    x_sem, z_sem, send_sem, recv_sem, halo_send, halo_recv, slab_send, slab_recv,
+    coeff_ref, index_ref, spectrum_ref, row_ref, class_ref, x_ref, z_ref, wave_ref, mode_ref, send_ref, recv_ref, pair_ref, poly_ref, even_ref, odd_ref, glow_ref, field_ref, light_ref, pack_ref, halo_ref, slab_ref,
+    in_sem, x_sem, z_sem, send_sem, recv_sem, halo_send, halo_recv, slab_send, slab_recv,
 ):
     me = lax.axis_index("depth")
     plane = lax.axis_index("plane")
@@ -198,11 +198,19 @@
         return pltpu.make_async_copy(x_hbm.at[half], x_ref.at[half], x_sem.at[step])
 
     z_copy = pltpu.make_async_copy(z_hbm, z_ref, z_sem)
+    spectrum_copy = pltpu.make_async_copy(spectrum_hbm, spectrum_ref, in_sem.at[0])
+    small_copies = [
+        pltpu.make_async_copy(coeff_hbm, coeff_ref, in_sem.at[1]),
+        pltpu.make_async_copy(index_hbm, index_ref, in_sem.at[2]),
+    ]
+    spectrum_copy.start()
 
     for step in range(2):
         x_copy(step).start()
 
     z_copy.start()
+    for copy in small_copies:
+        copy.start()
 
     barrier = pltpu.get_barrier_semaphore()
 
@@ -228,6 +236,7 @@
     def mode_keep():
         return pltpu.make_async_copy(send_ref.at[me], recv_ref.at[me], recv_sem.at[me])
 
+    spectrum_copy.wait()
     row_ref[...] = spectrum_ref[...].reshape(256, NX)
     gather_classes(row_ref, class_ref)
 
@@ -277,6 +286,8 @@
                 def _():
                     mode_keep().start()
 
+    for copy in small_copies:
+        copy.wait()
     fill_polynomials(coefficients(coeff_ref, index_ref), poly_ref)
 
     @pl.loop(0, 8)
@@ -348,6 +359,10 @@
 
     slab_keep.start()
 
+    @pl.loop(1, 32)
+    def _(step):
+        slab_send_copy(lax.rem(me + step, 32)).start()
+
     def evaluate(block, to_ref):
         rows = pl.ds(pl.multiple_of(jnp.minimum(block, 15) * 16, 16), 16)
         for pair in range(2):
@@ -367,18 +382,34 @@
         weight = through * opacity(depth)
         return weight, through - weight, depth_sum + depth
 
-    def in_pairs(start, cells, slabs):
+    def join_slabs(g):
+        for r in range(4):
+            parts = [slab_ref[g * 4 + d, r] for d in range(4)]
+            for y in range(4):
+                field_out[pl.ds(r * 32 + g * 4 + y, 8, stride=128), :] = shuffle(parts, y)
+
+    def in_pairs(start, cells, join):
         def step(n, state):
             block = start + 2 * n
-            if slabs:
-                @pl.loop(0, 8)
-                def _(k):
-                    @pl.when(4 * block + k > 0)
+            groups = [lax.rem(me // 4 + 15 - 2 * n - k, 8) for k in range(2)] if join else []
+            for g in groups:
+
+                @pl.loop(0, 4)
+                def _(d):
+                    source = 4 * g + d
+
+                    @pl.when(source != me)
                     def _():
-                        slab_send_copy(lax.rem(me + 4 * block + k, 32)).start()
+                        slab_recv_copy(source).wait_recv()
+
+                    @pl.when(source == me)
+                    def _():
+                        slab_keep.wait()
 
             evaluate(block + 1, odd_ref)
             state = cells(block, even_ref, state)
+            for g in groups:
+                join_slabs(g)
             evaluate(block + 2, even_ref)
             return cells(block + 1, odd_ref, state)
 
@@ -395,7 +426,7 @@
 
     zero = jnp.zeros((8, 128), f32)
     evaluate(0, even_ref)
-    through, depth_sum = lax.fori_loop(0, 4, in_pairs(0, front, True), (zero + 1.0, zero))
+    through, depth_sum = lax.fori_loop(0, 4, in_pairs(0, front, False), (zero + 1.0, zero))
 
     for halo in halos:
         halo.wait_recv()
@@ -427,24 +458,11 @@
                     colors[j] = colors[j] + weight * cell_depths(from_ref, r, k, j)
         return (*colors, through, depth_sum)
 
-    c0, c1, c2, _, depth_sum = lax.fori_loop(0, 4, in_pairs(8, back, False), (*colors, through, depth_sum))
+    c0, c1, c2, _, depth_sum = lax.fori_loop(0, 4, in_pairs(8, back, True), (*colors, through, depth_sum))
     for channel, image in enumerate((c0, c1, c2, jnp.exp(depth_sum * -tau_scale))):
         for y in range(4):
             moved = pltpu.roll(image, 128 - 32 * y, 1) if y else image
             image_out[pl.ds(channel * 4 + y, 8, stride=16), :] = moved
-
-    slab_keep.wait()
-
-    @pl.loop(1, 32)
-    def _(step):
-        slab_recv_copy(lax.rem(me + step, 32)).wait_recv()
-
-    @pl.loop(0, 8)
-    def _(g):
-        for r in range(4):
-            parts = [slab_ref[g * 4 + d, r] for d in range(4)]
-            for y in range(4):
-                field_out[pl.ds(r * 32 + g * 4 + y, 8, stride=128), :] = shuffle(parts, y)
 
     @pl.loop(1, 32)
     def _(step):
@@ -457,16 +475,18 @@
 
 
 def body(x_tab, z_tab, spectrum, transfer_coeffs, transfer_index):
-    smem = pl.BlockSpec(memory_space=pltpu.SMEM)
     vmem = pl.BlockSpec(memory_space=pltpu.VMEM)
     hbm = pl.BlockSpec(memory_space=pl.ANY)
     sem = pltpu.SemaphoreType.DMA
     field, image = pl.pallas_call(
         kernel,
         out_shape=[jax.ShapeDtypeStruct((1024, 128), f32), jax.ShapeDtypeStruct((128, 128), f32)],
-        in_specs=[smem, smem, vmem, hbm, hbm],
+        in_specs=[hbm] * 5,
         out_specs=[vmem, vmem],
         scratch_shapes=[
+            pltpu.SMEM((4, 4, 8), f32),
+            pltpu.SMEM((8,), jnp.int32),
+            pltpu.VMEM((2, 32, 4, NX), bf16),
             pltpu.VMEM((256, NX), bf16),
             pltpu.VMEM((4, 256, 256), bf16),
             pltpu.VMEM((2, 2, 4, 256, 256), bf16),
@@ -485,7 +505,7 @@
             pltpu.VMEM((2, 256, 128), f32),
             pltpu.VMEM((2, 256, 128), f32),
             pltpu.VMEM((32, 4, 8, 128), f32),
-            sem((2,)), sem, sem((32,)), sem((32,)), sem((2,)), sem((2,)), sem((32,)), sem((32,)),
+            sem((3,)), sem((2,)), sem, sem((32,)), sem((32,)), sem((2,)), sem((2,)), sem((32,)), sem((32,)),
         ],
         compiler_params=pltpu.CompilerParams(
             collective_id=0, has_side_effects=True, vmem_limit_bytes=60 * 2**20

time: 43.8 us -> 41.7 us (0.952)
  Pallas kernels: 39.6 us -> 37.5 us
    pallas_call x1, Pallas kernels: 39.6 us -> 37.5 us  [body(): pl.pallas_call(kernel, out_shape=[jax.ShapeDtypeStruct((1024, 128), f32),...]
where the time goes in v5:
time: 41.7 us; the launch traced here: 41.5 us
  Pallas kernels  37.5 us (90%)
  local copies, waits for them, and re-layouts  3.34 us (8%)
  between operations  0.64 us (2%)
    pallas_call x1, Pallas kernels, body(): pl.pallas_call(kernel, out_shape=[jax.ShapeDtypeStruct((1024, 128), f32),...  37.5 us
    unnamed x2, local copies, waits for them, and re-layouts  3.34 us

profile of v5, /device:TPU:1, one launch (start us, length us, event | category | flops | bytes accessed | tf_op | source)
XLA Modules:
  0.0 41.5 jit_solution(16128252158884755783)
XLA Ops:
  0.6 37.5 %shard_map.68 = (f32[1024,128]{1,0:T(8,128)}, f32[128,128]{1,0:T(8,128)}) custom-call(f32[4,4,8]{2,1,0:T(4,128)} %bitcast.10, s32[8]{0:T(128)} %index_hbm.1, bf16[2,32,4,1024]{3,2,1,0:T(4,128)(2,1)} %spectrum_hbm.1, bf16[2,2,4,256,256]{4,3,2,1,0:T(8,128)(2,1)} %constant.4.clone.x_hbm, bf16[4,512,512]{2,1,0:T(8,128)(2,1)} %constant.5.clone.z_hbm), custom_call_target="tpu_custom_call" | custom-call | tf_op jit(solution)/shard_map/pallas_call | solution.py:481
  38.1 1.9 %copy.10 = f32[32,4,1024]{2,1,0:T(4,128)} copy(f32[32,4,1024]{2,1,0:T(4,128)} %bitcast.8) | data formatting | bytes 1048576
  40.0 1.5 %copy.11 = f32[8,4,4,32]{3,2,1,0:T(4,128)} copy(f32[8,4,4,32]{3,2,1,0:T(4,128)} %bitcast.9) | data formatting | bytes 32768

commit v6 on v5

--- a/solution.py
+++ b/solution.py
@@ -14,6 +14,7 @@
 density = 2.0
 shade_gain = 0.4
 tau_scale = density / NZ
+LN2 = math.log(2.0)
 f32 = jnp.float32
 bf16 = jnp.bfloat16
 MESH = pl.DeviceIdType.MESH
@@ -114,14 +115,14 @@
 
 
 def softplus(p):
-    return jnp.maximum(p, jnp.log(1.0 + jnp.exp(jnp.minimum(p, 80.0))))
+    return jnp.maximum(p, jnp.log2(1.0 + jnp.exp2(jnp.minimum(p, 120.0))))
 
 
 def opacity(depth):
-    k1, k2, k3 = tau_scale, tau_scale**2 / 2, tau_scale**3 / 6
-    small = depth * (k1 - depth * (k2 - depth * k3))
-    large = 1.0 - jnp.exp2(depth * (-tau_scale / math.log(2.0)))
-    return jnp.where(depth < 16.0, small, large)
+    k = LN2 * tau_scale
+    small = depth * (k - depth * (k * k / 2))
+    large = 1.0 - jnp.exp2(depth * -tau_scale)
+    return jnp.where(depth < 2.5, small, large)
 
 
 def pieces(value, count):
@@ -139,9 +140,9 @@
     for channel in range(4):
         terms = []
         for n in (1, 2, 3):
-            high, low = (piece.astype(f32) for piece in pieces(coeffs[4 * channel + n], 2))
+            high, low = (piece.astype(f32) for piece in pieces(coeffs[4 * channel + n] * (1.0 / LN2), 2))
             terms += [high, high, low, low]
-        terms += [piece.astype(f32) for piece in pieces(coeffs[4 * channel], 3)] + [jnp.zeros((8, 128), f32)]
+        terms += [piece.astype(f32) for piece in pieces(coeffs[4 * channel] * (1.0 / LN2), 3)] + [jnp.zeros((8, 128), f32)]
         for tile in range(2):
             value = terms[8 * tile]
             for t in range(1, 8):
@@ -377,10 +378,9 @@
         rows = pl.ds(pl.multiple_of(block * 16, 16), 16)
         return jnp.broadcast_to(light_ref[r, rows, :][k : k + 1, :], (8, 128))
 
-    def absorb(from_ref, r, k, through, depth_sum):
-        depth = cell_depths(from_ref, r, k, 3)
-        weight = through * opacity(depth)
-        return weight, through - weight, depth_sum + depth
+    def absorb(from_ref, r, k, through):
+        weight = through * opacity(cell_depths(from_ref, r, k, 3))
+        return weight, through - weight
 
     def join_slabs(g):
         for r in range(4):
@@ -388,10 +388,10 @@
             for y in range(4):
                 field_out[pl.ds(r * 32 + g * 4 + y, 8, stride=128), :] = shuffle(parts, y)
 
-    def in_pairs(start, cells, join):
+    def in_fours(start, cells, join):
         def step(n, state):
-            block = start + 2 * n
-            groups = [lax.rem(me // 4 + 15 - 2 * n - k, 8) for k in range(2)] if join else []
+            block = start + 4 * n
+            groups = [lax.rem(me // 4 + 15 - 4 * n - k, 8) for k in range(4)] if join else []
             for g in groups:
 
                 @pl.loop(0, 4)
@@ -406,27 +406,28 @@
                     def _():
                         slab_keep.wait()
 
-            evaluate(block + 1, odd_ref)
-            state = cells(block, even_ref, state)
-            for g in groups:
-                join_slabs(g)
-            evaluate(block + 2, even_ref)
-            return cells(block + 1, odd_ref, state)
+            for k in range(4):
+                here, ahead = (even_ref, odd_ref) if k % 2 == 0 else (odd_ref, even_ref)
+                evaluate(block + k + 1, ahead)
+                state = cells(block + k, here, state)
+                for g in groups[k : k + 1]:
+                    join_slabs(g)
+            return state
 
         return step
 
     def front(block, from_ref, state):
-        through, depth_sum = state
+        through = state
         for k in range(16):
             for r in range(4):
-                weight, through, depth_sum = absorb(from_ref, r, k, through, depth_sum)
+                weight, through = absorb(from_ref, r, k, through)
                 for j in range(3):
                     glow_ref[block, 4 * k + r, j] = weight * cell_depths(from_ref, r, k, j)
-        return through, depth_sum
+        return through
 
     zero = jnp.zeros((8, 128), f32)
     evaluate(0, even_ref)
-    through, depth_sum = lax.fori_loop(0, 4, in_pairs(0, front, False), (zero + 1.0, zero))
+    through = lax.fori_loop(0, 2, in_fours(0, front, False), zero + 1.0)
 
     for halo in halos:
         halo.wait_recv()
@@ -449,17 +450,17 @@
     colors = lax.fori_loop(0, 8, lit, (zero, zero, zero))
 
     def back(block, from_ref, state):
-        *colors, through, depth_sum = state
+        *colors, through = state
         for k in range(16):
             for r in range(4):
-                weight, through, depth_sum = absorb(from_ref, r, k, through, depth_sum)
+                weight, through = absorb(from_ref, r, k, through)
                 weight = weight * cell_light(block, r, k)
                 for j in range(3):
                     colors[j] = colors[j] + weight * cell_depths(from_ref, r, k, j)
-        return (*colors, through, depth_sum)
-
-    c0, c1, c2, _, depth_sum = lax.fori_loop(0, 4, in_pairs(8, back, True), (*colors, through, depth_sum))
-    for channel, image in enumerate((c0, c1, c2, jnp.exp(depth_sum * -tau_scale))):
+        return (*colors, through)
+
+    *colors, through = lax.fori_loop(0, 2, in_fours(8, back, True), (*colors, through))
+    for channel, image in enumerate([color * LN2 for color in colors] + [through]):
         for y in range(4):
             moved = pltpu.roll(image, 128 - 32 * y, 1) if y else image
             image_out[pl.ds(channel * 4 + y, 8, stride=16), :] = moved
@@ -508,7 +509,7 @@
             sem((3,)), sem((2,)), sem, sem((32,)), sem((32,)), sem((2,)), sem((2,)), sem((32,)), sem((32,)),
         ],
         compiler_params=pltpu.CompilerParams(
-            collective_id=0, has_side_effects=True, vmem_limit_bytes=60 * 2**20
+            collective_id=0, has_side_effects=True, vmem_limit_bytes=53 * 2**20
         ),
     )(transfer_coeffs.transpose(1, 2, 0), transfer_index, spectrum, x_tab, z_tab)
     scalar_field = field.reshape(32, 8, 4, 128).transpose(0, 2, 1, 3).reshape(32, 4, NX)

time: 41.7 us -> 38.4 us (0.921)
  Pallas kernels: 37.5 us -> 34.9 us
  local copies, waits for them, and re-layouts: 3.34 us -> 2.77 us
    pallas_call x1, Pallas kernels: 37.5 us -> 34.9 us  [body(): pl.pallas_call(kernel, out_shape=[jax.ShapeDtypeStruct((1024, 128), f32),...]
    unnamed x2 -> x6, local copies, waits for them, and re-layouts: 3.34 us -> 2.77 us
where the time goes in v6:
time: 38.4 us; the launch traced here: 38.3 us
  Pallas kernels  34.9 us (91%)
  local copies, waits for them, and re-layouts  2.77 us (7%)
  between operations  0.65 us (2%)
    pallas_call x1, Pallas kernels, body(): pl.pallas_call(kernel, out_shape=[jax.ShapeDtypeStruct((1024, 128), f32),...  34.9 us
    unnamed x6, local copies, waits for them, and re-layouts  2.77 us

profile of v6, /device:TPU:1, one launch (start us, length us, event | category | flops | bytes accessed | tf_op | source)
XLA Modules:
  0.0 38.3 jit_solution(11131665977154852279)
XLA Ops:
  0.6 0.0 copy-start
  0.6 0.7 %copy-done = f32[8,4,4]{0,2,1:T(4,128)S(1)} copy-done((f32[8,4,4]{0,2,1:T(4,128)S(1)}, f32[8,4,4]{0,2,1:T(4,128)}, u32[]{:S(2)}) %copy-start) | copy-done | bytes 536
  1.3 0.0 copy-start.1
  1.3 0.7 %copy-done.1 = s32[8]{0:T(128)S(1)} copy-done((s32[8]{0:T(128)S(1)}, s32[8]{0:T(128)}, u32[]{:S(2)}) %copy-start.1) | copy-done | bytes 56
  2.0 34.9 %shard_map.68 = (f32[1024,128]{1,0:T(8,128)S(1)}, f32[128,128]{1,0:T(8,128)S(1)}) custom-call(f32[4,4,8]{2,1,0:T(4,128)S(1)} %bitcast.10, s32[8]{0:T(128)S(1)} %copy-done.1, bf16[2,32,4,1024]{3,2,1,0:T(4,128)(2,1)} %spectrum_hbm.1, bf16[2,2,4,256,256]{4,3,2,1,0:T(8,128)(2,1)} %constant.4.clone.x_hbm, bf16[4,512,512]{2,1,0:T(8,128)(2,1)} %constant.5.clone.z_hbm), custom_call_target="tpu_custom_call" | custom-call | tf_op jit(solution)/shard_map/pallas_call | solution.py:482
  36.9 0.8 %copy.10 = f32[32,4,1024]{2,1,0:T(4,128)} copy(f32[32,4,1024]{2,1,0:T(4,128)S(1)} %bitcast.8) | data formatting | bytes 1048576
  37.7 0.6 %copy.11 = f32[8,4,4,32]{3,2,1,0:T(4,128)} copy(f32[8,4,4,32]{3,2,1,0:T(4,128)S(1)} %bitcast.9) | data formatting | bytes 32768
Async XLA Ops:
  0.6 0.7 %copy-start = (f32[8,4,4]{0,2,1:T(4,128)S(1)}, f32[8,4,4]{0,2,1:T(4,128)}, u32[]{:S(2)}) copy-start(f32[8,4,4]{0,2,1:T(4,128)} %param.6) | copy-start | bytes 1540
  1.3 0.7 %copy-start.1 = (s32[8]{0:T(128)S(1)}, s32[8]{0:T(128)}, u32[]{:S(2)}) copy-start(s32[8]{0:T(128)} %index_hbm.1) | copy-start | bytes 100

commit v7 on v6

--- a/solution.py
+++ b/solution.py
@@ -391,7 +391,7 @@
     def in_fours(start, cells, join):
         def step(n, state):
             block = start + 4 * n
-            groups = [lax.rem(me // 4 + 15 - 4 * n - k, 8) for k in range(4)] if join else []
+            groups = [lax.rem(me // 4 + 15 - k, 8) for k in range(8)] if join else []
             for g in groups:
 
                 @pl.loop(0, 4)
@@ -410,7 +410,7 @@
                 here, ahead = (even_ref, odd_ref) if k % 2 == 0 else (odd_ref, even_ref)
                 evaluate(block + k + 1, ahead)
                 state = cells(block + k, here, state)
-                for g in groups[k : k + 1]:
+                for g in groups[2 * k : 2 * k + 2]:
                     join_slabs(g)
             return state
 
@@ -427,14 +427,14 @@
 
     zero = jnp.zeros((8, 128), f32)
     evaluate(0, even_ref)
-    through = lax.fori_loop(0, 2, in_fours(0, front, False), zero + 1.0)
+    through = lax.fori_loop(0, 3, in_fours(0, front, False), zero + 1.0)
 
     for halo in halos:
         halo.wait_recv()
 
-    @pl.loop(0, 8)
+    @pl.loop(0, 4)
     def _(step):
-        rows = pl.ds(pl.multiple_of(step * 32, 32), 32)
+        rows = pl.ds(pl.multiple_of(step * 64, 64), 64)
         for r in range(4):
             light_ref[r, rows, :] = lighting(field_ref[r, rows, :], halo_ref[0, rows, :], halo_ref[1, rows, :], r)
 
@@ -447,7 +447,7 @@
                     colors[j] = colors[j] + light * glow_ref[block, 4 * k + r, j]
         return tuple(colors)
 
-    colors = lax.fori_loop(0, 8, lit, (zero, zero, zero))
+    colors = lax.fori_loop(0, 12, lit, (zero, zero, zero))
 
     def back(block, from_ref, state):
         *colors, through = state
@@ -459,7 +459,7 @@
                     colors[j] = colors[j] + weight * cell_depths(from_ref, r, k, j)
         return (*colors, through)
 
-    *colors, through = lax.fori_loop(0, 2, in_fours(8, back, True), (*colors, through))
+    *colors, through = in_fours(12, back, True)(0, (*colors, through))
     for channel, image in enumerate([color * LN2 for color in colors] + [through]):
         for y in range(4):
             moved = pltpu.roll(image, 128 - 32 * y, 1) if y else image
@@ -500,7 +500,7 @@
             pltpu.VMEM((512, 256), bf16),
             pltpu.VMEM((2, 512, 256), f32),
             pltpu.VMEM((2, 512, 256), f32),
-            pltpu.VMEM((8, 64, 3, 8, 128), f32),
+            pltpu.VMEM((12, 64, 3, 8, 128), f32),
             pltpu.VMEM((4, 256, 128), f32),
             pltpu.VMEM((4, 256, 128), f32),
             pltpu.VMEM((2, 256, 128), f32),

time: 38.4 us -> 36.8 us (0.958)
  Pallas kernels: 34.9 us -> 33.2 us
    pallas_call x1, Pallas kernels: 34.9 us -> 33.2 us  [body(): pl.pallas_call(kernel, out_shape=[jax.ShapeDtypeStruct((1024, 128), f32),...]
where the time goes in v7:
time: 36.8 us; the launch traced here: 36.6 us
  Pallas kernels  33.2 us (90%)
  local copies, waits for them, and re-layouts  2.77 us (8%)
  between operations  0.65 us (2%)
    pallas_call x1, Pallas kernels, body(): pl.pallas_call(kernel, out_shape=[jax.ShapeDtypeStruct((1024, 128), f32),...  33.2 us
    unnamed x6, local copies, waits for them, and re-layouts  2.77 us

profile of v7, /device:TPU:1, one launch (start us, length us, event | category | flops | bytes accessed | tf_op | source)
XLA Modules:
  0.0 36.6 jit_solution(15663933800403435667)
XLA Ops:
  0.6 0.0 copy-start
  0.6 0.7 %copy-done = f32[8,4,4]{0,2,1:T(4,128)S(1)} copy-done((f32[8,4,4]{0,2,1:T(4,128)S(1)}, f32[8,4,4]{0,2,1:T(4,128)}, u32[]{:S(2)}) %copy-start) | copy-done | bytes 536
  1.3 0.0 copy-start.1
  1.3 0.7 %copy-done.1 = s32[8]{0:T(128)S(1)} copy-done((s32[8]{0:T(128)S(1)}, s32[8]{0:T(128)}, u32[]{:S(2)}) %copy-start.1) | copy-done | bytes 56
  2.0 33.2 %shard_map.68 = (f32[1024,128]{1,0:T(8,128)S(1)}, f32[128,128]{1,0:T(8,128)S(1)}) custom-call(f32[4,4,8]{2,1,0:T(4,128)S(1)} %bitcast.10, s32[8]{0:T(128)S(1)} %copy-done.1, bf16[2,32,4,1024]{3,2,1,0:T(4,128)(2,1)} %spectrum_hbm.1, bf16[2,2,4,256,256]{4,3,2,1,0:T(8,128)(2,1)} %constant.4.clone.x_hbm, bf16[4,512,512]{2,1,0:T(8,128)(2,1)} %constant.5.clone.z_hbm), custom_call_target="tpu_custom_call" | custom-call | tf_op jit(solution)/shard_map/pallas_call | solution.py:482
  35.2 0.8 %copy.10 = f32[32,4,1024]{2,1,0:T(4,128)} copy(f32[32,4,1024]{2,1,0:T(4,128)S(1)} %bitcast.8) | data formatting | bytes 1048576
  36.0 0.6 %copy.11 = f32[8,4,4,32]{3,2,1,0:T(4,128)} copy(f32[8,4,4,32]{3,2,1,0:T(4,128)S(1)} %bitcast.9) | data formatting | bytes 32768
Async XLA Ops:
  0.6 0.7 %copy-start = (f32[8,4,4]{0,2,1:T(4,128)S(1)}, f32[8,4,4]{0,2,1:T(4,128)}, u32[]{:S(2)}) copy-start(f32[8,4,4]{0,2,1:T(4,128)} %param.6) | copy-start | bytes 1540
  1.3 0.7 %copy-start.1 = (s32[8]{0:T(128)S(1)}, s32[8]{0:T(128)}, u32[]{:S(2)}) copy-start(s32[8]{0:T(128)} %index_hbm.1) | copy-start | bytes 100

commit v8 on v7

--- a/solution.py
+++ b/solution.py
@@ -319,8 +319,7 @@
 
     z_copy.wait()
 
-    @pl.loop(0, 4)
-    def _(r):
+    for r in range(4):
         p = dot(z_ref[r], pair_ref[r])
         field_ref[r] = (p[:256, :128] + p[:256, 128:]) + (p[256:, :128] + p[256:, 128:])
 
@@ -444,10 +443,12 @@
             for r in range(4):
                 light = cell_light(block, r, k)
                 for j in range(3):
-                    colors[j] = colors[j] + light * glow_ref[block, 4 * k + r, j]
+                    n = j + 3 * (r % 2)
+                    colors[n] = colors[n] + light * glow_ref[block, 4 * k + r, j]
         return tuple(colors)
 
-    colors = lax.fori_loop(0, 12, lit, (zero, zero, zero))
+    colors = lax.fori_loop(0, 12, lit, (zero,) * 6)
+    colors = [colors[j] + colors[j + 3] for j in range(3)]
 
     def back(block, from_ref, state):
         *colors, through = state

time: 36.8 us -> 36.1 us (0.981)
  Pallas kernels: 33.2 us -> 32.5 us
    pallas_call x1, Pallas kernels: 33.2 us -> 32.5 us  [body(): pl.pallas_call(kernel, out_shape=[jax.ShapeDtypeStruct((1024, 128), f32),...]
where the time goes in v8:
time: 36.1 us; the launch traced here: 35.9 us
  Pallas kernels  32.5 us (90%)
  local copies, waits for them, and re-layouts  2.77 us (8%)
  between operations  0.65 us (2%)
    pallas_call x1, Pallas kernels, body(): pl.pallas_call(kernel, out_shape=[jax.ShapeDtypeStruct((1024, 128), f32),...  32.5 us
    unnamed x6, local copies, waits for them, and re-layouts  2.77 us

profile of v8, /device:TPU:1, one launch (start us, length us, event | category | flops | bytes accessed | tf_op | source)
XLA Modules:
  0.0 35.9 jit_solution(962710740060327699)
XLA Ops:
  0.6 0.0 copy-start
  0.6 0.7 %copy-done = f32[8,4,4]{0,2,1:T(4,128)S(1)} copy-done((f32[8,4,4]{0,2,1:T(4,128)S(1)}, f32[8,4,4]{0,2,1:T(4,128)}, u32[]{:S(2)}) %copy-start) | copy-done | bytes 536
  1.3 0.0 copy-start.1
  1.3 0.7 %copy-done.1 = s32[8]{0:T(128)S(1)} copy-done((s32[8]{0:T(128)S(1)}, s32[8]{0:T(128)}, u32[]{:S(2)}) %copy-start.1) | copy-done | bytes 56
  2.0 32.5 %shard_map.68 = (f32[1024,128]{1,0:T(8,128)S(1)}, f32[128,128]{1,0:T(8,128)S(1)}) custom-call(f32[4,4,8]{2,1,0:T(4,128)S(1)} %bitcast.10, s32[8]{0:T(128)S(1)} %copy-done.1, bf16[2,32,4,1024]{3,2,1,0:T(4,128)(2,1)} %spectrum_hbm.1, bf16[2,2,4,256,256]{4,3,2,1,0:T(8,128)(2,1)} %constant.4.clone.x_hbm, bf16[4,512,512]{2,1,0:T(8,128)(2,1)} %constant.5.clone.z_hbm), custom_call_target="tpu_custom_call" | custom-call | tf_op jit(solution)/shard_map/pallas_call | solution.py:483
  34.5 0.8 %copy.10 = f32[32,4,1024]{2,1,0:T(4,128)} copy(f32[32,4,1024]{2,1,0:T(4,128)S(1)} %bitcast.8) | data formatting | bytes 1048576
  35.3 0.6 %copy.11 = f32[8,4,4,32]{3,2,1,0:T(4,128)} copy(f32[8,4,4,32]{3,2,1,0:T(4,128)S(1)} %bitcast.9) | data formatting | bytes 32768
Async XLA Ops:
  0.6 0.7 %copy-start = (f32[8,4,4]{0,2,1:T(4,128)S(1)}, f32[8,4,4]{0,2,1:T(4,128)}, u32[]{:S(2)}) copy-start(f32[8,4,4]{0,2,1:T(4,128)} %param.6) | copy-start | bytes 1540
  1.3 0.7 %copy-start.1 = (s32[8]{0:T(128)S(1)}, s32[8]{0:T(128)}, u32[]{:S(2)}) copy-start(s32[8]{0:T(128)} %index_hbm.1) | copy-start | bytes 100
